TPU v7x, 512 devices: a whole 4x4x16 slice. The times are simulated.
512 devices in a mesh: kv: 64 (over x, z), head: 8 (over y, core).
Axes of the slice: x: 4, y: 4, z: 16, core: 2. Of those that a mesh axis runs over, the one named last changes fastest.
Arguments:
- query_nope: bfloat16 [2, 8, 128, 128], P(None, None, 'head'), may hold values from -6 to 6
- query_rope: bfloat16 [2, 8, 128, 64], P(None, None, 'head'), may hold values from -56 to 56
- new_latent: bfloat16 [2, 8, 512], P(None, None, 'head'), may hold values from -6 to 6
- new_rope: bfloat16 [2, 8, 64], P(None, None, 'head'), may hold values from -9 to 9
- cache_latent: bfloat16 [8, 16384, 512], P(None, 'kv'), may hold values from -6 to 6
- cache_rope: bfloat16 [8, 64, 16384], P(None, None, 'kv'), may hold values from -5 to 5
- lengths: int32 [8], replicated, may hold values from 2048 to 16382
- uk_weight: bfloat16 [128, 128, 512], P('head', None, 'kv'), may hold values from -0.5 to 0.5
- uv_weight: bfloat16 [128, 512, 128], P('head'), may hold values from -0.25 to 0.25
Outputs:
- attended: bfloat16 [2, 1024, 128], P(None, ('head', 'kv'))
All inputs are finite; a program needn't handle non-finite values.
Results may differ from a plain program's by a relative error of at most 0.0072.
Values may be sent and summed in bfloat16 or wider, within the bound.
No kernel may reach another device: no remote copies, remote signals or barrier semaphores. Data moves between devices by JAX's collectives and lax.ppermute only.
A program may use at most 64 MiB of HBM per device.

v0:
```python
import math

import jax
import jax.numpy as jnp
from jax import lax
from jax.sharding import PartitionSpec as P

mscale = (0.1 * math.log(40.0) + 1.0) ** 2


def on_device(
    query_nope,
    query_rope,
    new_latent,
    new_rope,
    cache_latent,
    cache_rope,
    lengths,
    uk_weight,
    uv_weight,
):
    single = jnp.float32
    narrow = jnp.bfloat16
    exact = lax.Precision.HIGHEST
    kv_count = lax.axis_size("kv")
    kv_index = lax.axis_index("kv")
    step_count, requests, heads_loc, nope_dim = query_nope.shape
    pos_dev = cache_latent.shape[1]
    latent = uv_weight.shape[1]
    softmax_scale = mscale / math.sqrt(nope_dim + query_rope.shape[3])
    item_count = heads_loc * requests
    per_dev = item_count // kv_count
    latent_part = jnp.einsum(
        "sbhn,hnl->sbhl", query_nope, uk_weight, preferred_element_type=single
    ).astype(narrow)
    gathered_latent, key_rope = (
        lax.all_gather(new_latent, "head", axis=2, tiled=True),
        lax.all_gather(new_rope, "head", axis=2, tiled=True),
    )
    raw_keys = gathered_latent.astype(single)
    key_latent = (
        raw_keys * lax.rsqrt(jnp.mean(raw_keys * raw_keys, axis=-1, keepdims=True) + 1e-06)
    ).astype(narrow)
    places = kv_index * pos_dev + lax.iota(jnp.int32, pos_dev)
    live_mask = places[None, :] < lengths[:, None]
    fresh_places = lengths[None, :] + lax.iota(jnp.int32, step_count)[:, None]
    owner_mask = jnp.transpose(fresh_places // pos_dev == kv_index)

    def add_columns(running, block_piece):
        return (
            running[0]
            + jnp.einsum(
                "sbhl,bjl->shbj", block_piece, cache_latent, preferred_element_type=single
            ),
            running[1]
            + jnp.einsum("sbhl,tbl->shbt", block_piece, key_latent, preferred_element_type=single),
        )

    def owner_project(merged):
        first_item = kv_index * per_dev
        head_weight = lax.dynamic_index_in_dim(
            uv_weight, first_item // requests, 0, keepdims=False
        ).astype(single)
        return jnp.einsum("sil,lv->siv", merged, head_weight, precision=exact)

    def combine(mixture, highest, totals, block_steps):
        received, part_peaks, part_totals = (
            lax.all_to_all(mixture, "kv", split_axis=1, concat_axis=1, tiled=True),
            lax.all_to_all(highest, "kv", split_axis=1, concat_axis=1, tiled=True),
            lax.all_to_all(totals, "kv", split_axis=1, concat_axis=1, tiled=True),
        )
        width = received.shape[2]
        received = received.reshape(block_steps, kv_count, per_dev, width)
        part_peaks = part_peaks.reshape(block_steps, kv_count, per_dev)
        part_totals = part_totals.reshape(block_steps, kv_count, per_dev)
        summit = jnp.max(part_peaks, axis=1, keepdims=True)
        factor = jnp.exp(part_peaks - summit)
        merged_sum = jnp.sum(received * factor[..., None], axis=1)
        merged_total = jnp.sum(part_totals * factor, axis=1)
        projected = owner_project(merged_sum) / merged_total[..., None]
        return projected.astype(narrow)

    def attend(first_step, block_steps):
        pieces = lax.slice_in_dim(latent_part, first_step, first_step + block_steps, axis=0)
        rotary = lax.slice_in_dim(query_rope, first_step, first_step + block_steps, axis=0)
        cached = jnp.einsum("sbhr,brj->shbj", rotary, cache_rope, preferred_element_type=single)
        fresh_scores = jnp.einsum("sbhr,tbr->shbt", rotary, key_rope, preferred_element_type=single)
        cached, fresh_scores = add_columns(
            (cached, fresh_scores), lax.all_gather(pieces, "kv", axis=3, tiled=True)
        )
        allowed = (
            lax.iota(jnp.int32, step_count)[None, :]
            <= (first_step + lax.iota(jnp.int32, block_steps))[:, None]
        )
        fresh_mask = allowed[:, None, None, :] & owner_mask[None, None, :, :]
        cached = jnp.where(live_mask[None, None], cached * softmax_scale, -1e30)
        fresh_scores = jnp.where(fresh_mask, fresh_scores * softmax_scale, -1e30)
        highest = jnp.maximum(jnp.max(cached, axis=-1), jnp.max(fresh_scores, axis=-1))
        weights = jnp.where(
            live_mask[None, None], jnp.exp(cached - highest[..., None]), 0.0
        ).astype(narrow)
        fresh_weights = jnp.where(
            fresh_mask, jnp.exp(fresh_scores - highest[..., None]), 0.0
        ).astype(narrow)
        totals = jnp.sum(weights, axis=-1, dtype=single) + jnp.sum(
            fresh_weights, axis=-1, dtype=single
        )
        mixture = jnp.einsum("shbj,bjl->shbl", weights, cache_latent, preferred_element_type=single)
        mixture = mixture + jnp.einsum(
            "shbt,tbl->shbl", fresh_weights, key_latent, preferred_element_type=single
        )
        return combine(
            mixture.reshape(block_steps, item_count, latent),
            highest.reshape(block_steps, item_count),
            totals.reshape(block_steps, item_count),
            block_steps,
        )

    result = jnp.concatenate([attend(step_id, 1) for step_id in range(step_count)], axis=0)
    return result


def solution(mesh):
    return jax.shard_map(
        on_device,
        mesh=mesh,
        in_specs=(
            P(None, None, "head", None),
            P(None, None, "head", None),
            P(None, None, "head"),
            P(None, None, "head"),
            P(None, "kv", None),
            P(None, None, "kv"),
            P(),
            P("head", None, "kv"),
            P("head", None, None),
        ),
        out_specs=P(None, ("head", "kv"), None),
        check_vma=False,
    )
```

profile of v0, /device:TPU:6, one launch (start us, length us, event | category | flops | bytes accessed | tf_op | source)
XLA Modules:
  0.0 407.9 jit_solution(12898074977291354625)
XLA Ops:
  0.0 0.9 copy.79
  0.9 13.3 %all_gather.13 = bf16[2,8,64]{1,0,2:T(2,128)(2,1)S(1)} all-gather(bf16[2,8,8]{1,0,2:T(2,128)(2,1)S(1)} %copy.79), channel_id=1, replica_groups=mesh['kv'=64,'head'=8] {'head'}, dimensions={2}, use_global_device_ids=true | all-gather | bytes 2304 | tf_op jit(solution)/shard_map/all_gather | solution.py:38
  14.3 0.9 fusion.39
  15.2 0.9 fusion.35
  16.1 1.1 fusion.41
  17.2 1.1 fusion.37
  18.4 0.8 copy.81
  19.2 12.8 %all_gather.14 = bf16[2,8,512]{1,0,2:T(2,128)(2,1)S(1)} all-gather(bf16[2,8,64]{1,0,2:T(2,128)(2,1)S(1)} %copy.81), channel_id=1, replica_groups=mesh['kv'=64,'head'=8] {'head'}, dimensions={2}, use_global_device_ids=true | all-gather | bytes 18432 | tf_op jit(solution)/shard_map/all_gather | solution.py:37
  32.3 1.3 fusion.12
  33.6 121.6 %all_gather.12 = bf16[1,8,16,512]{1,3,0,2:T(8,128)(2,1)} all-gather(bf16[1,8,16,8]{1,3,0,2:T(8,128)(2,1)S(1)} %get-tuple-element.11), channel_id=1, replica_groups=mesh['kv'=64,'head'=8] {'kv'}, dimensions={3}, use_global_device_ids=true | all-gather | bytes 133120 | tf_op jit(solution)/shard_map/all_gather | solution.py:89
  155.2 1.9 copy.78
  157.2 113.5 %all_gather.15 = bf16[1,8,16,512]{1,3,0,2:T(8,128)(2,1)} all-gather(bf16[1,8,16,8]{1,3,0,2:T(8,128)(2,1)S(1)} %get-tuple-element.12), channel_id=1, replica_groups=mesh['kv'=64,'head'=8] {'kv'}, dimensions={3}, use_global_device_ids=true | all-gather | bytes 133120 | tf_op jit(solution)/shard_map/all_gather | solution.py:89
  270.7 1.9 copy.94
  272.9 0.7 fusion.68
  273.7 0.7 fusion.66
  275.7 12.2 %all-to-all-start.2 = ((f32[1,64,2]{2,0,1:T(1,128)}), f32[1,64,2]{2,0,1:T(1,128)S(1)}, u32[]{:S(2)}, u32[]{:S(2)}) async-start(f32[1,64,2]{2,0,1:T(1,128)} %bitcast.20), calls=%async_computation.2 | async-start | bytes 65536 | tf_op jit(solution)/shard_map/all_to_all | solution.py:70
  288.6 12.0 %all-to-all-done.2 = f32[1,64,2]{2,0,1:T(1,128)S(1)} async-done(((f32[1,64,2]{2,0,1:T(1,128)}), f32[1,64,2]{2,0,1:T(1,128)S(1)}, u32[]{:S(2)}, u32[]{:S(2)}) %all-to-all-start.2) | async-done | bytes 544 | tf_op jit(solution)/shard_map/all_to_all | solution.py:70
  300.7 6.3 %all-to-all-start.1 = ((f32[1,64,2]{2,0,1:T(1,128)}), f32[1,64,2]{2,0,1:T(1,128)S(1)}, u32[]{:S(2)}, u32[]{:S(2)}) async-start(f32[1,64,2]{2,0,1:T(1,128)} %bitcast.17), calls=%async_computation.1 | async-start | bytes 65536 | tf_op jit(solution)/shard_map/all_to_all | solution.py:69
  307.8 12.1 %all-to-all-done.1 = f32[1,64,2]{2,0,1:T(1,128)S(1)} async-done(((f32[1,64,2]{2,0,1:T(1,128)}), f32[1,64,2]{2,0,1:T(1,128)S(1)}, u32[]{:S(2)}, u32[]{:S(2)}) %all-to-all-start.1) | async-done | bytes 544 | tf_op jit(solution)/shard_map/all_to_all | solution.py:69
  319.9 7.4 %all-to-all-start.5 = ((f32[1,64,2]{2,0,1:T(1,128)}), f32[1,64,2]{2,0,1:T(1,128)S(1)}, u32[]{:S(2)}, u32[]{:S(2)}) async-start(f32[1,64,2]{2,0,1:T(1,128)} %bitcast.38), calls=%async_computation.5 | async-start | bytes 65536 | tf_op jit(solution)/shard_map/all_to_all | solution.py:70
  327.8 0.7 max.43
  328.5 11.4 %all-to-all-done.5 = f32[1,64,2]{2,0,1:T(1,128)S(1)} async-done(((f32[1,64,2]{2,0,1:T(1,128)}), f32[1,64,2]{2,0,1:T(1,128)S(1)}, u32[]{:S(2)}, u32[]{:S(2)}) %all-to-all-start.5) | async-done | bytes 544 | tf_op jit(solution)/shard_map/all_to_all | solution.py:70
  339.9 6.3 %all-to-all-start.4 = ((f32[1,64,2]{2,0,1:T(1,128)}), f32[1,64,2]{2,0,1:T(1,128)S(1)}, u32[]{:S(2)}, u32[]{:S(2)}) async-start(f32[1,64,2]{2,0,1:T(1,128)} %bitcast.36), calls=%async_computation.4 | async-start | bytes 65536 | tf_op jit(solution)/shard_map/all_to_all | solution.py:69
  346.6 1.0 copy.87
  347.6 11.0 %all-to-all-done.4 = f32[1,64,2]{2,0,1:T(1,128)S(1)} async-done(((f32[1,64,2]{2,0,1:T(1,128)}), f32[1,64,2]{2,0,1:T(1,128)S(1)}, u32[]{:S(2)}, u32[]{:S(2)}) %all-to-all-start.4) | async-done | bytes 544 | tf_op jit(solution)/shard_map/all_to_all | solution.py:69
  358.5 6.5 %all-to-all-start = ((f32[1,128,512]{2,0,1:T(1,128)}), f32[1,128,512]{2,0,1:T(1,128)S(1)}, u32[]{:S(2)}, u32[]{:S(2)}) async-start(f32[1,128,512]{2,0,1:T(1,128)} %copy.87), calls=%async_computation | async-start | bytes 524288 | tf_op jit(solution)/shard_map/all_to_all | solution.py:68
  365.9 1.0 copy.100
  366.9 14.7 %all-to-all-done = f32[1,128,512]{2,0,1:T(1,128)S(1)} async-done(((f32[1,128,512]{2,0,1:T(1,128)}), f32[1,128,512]{2,0,1:T(1,128)S(1)}, u32[]{:S(2)}, u32[]{:S(2)}) %all-to-all-start) | async-done | bytes 262176 | tf_op jit(solution)/shard_map/all_to_all | solution.py:68
  381.6 6.7 %all-to-all-start.3 = ((f32[1,128,512]{2,0,1:T(1,128)}), f32[1,128,512]{2,0,1:T(1,128)S(1)}, u32[]{:S(2)}, u32[]{:S(2)}) async-start(f32[1,128,512]{2,0,1:T(1,128)} %copy.100), calls=%async_computation.3 | async-start | bytes 524288 | tf_op jit(solution)/shard_map/all_to_all | solution.py:68
  389.5 15.3 %all-to-all-done.3 = f32[1,128,512]{2,0,1:T(1,128)S(1)} async-done(((f32[1,128,512]{2,0,1:T(1,128)}), f32[1,128,512]{2,0,1:T(1,128)S(1)}, u32[]{:S(2)}, u32[]{:S(2)}) %all-to-all-start.3) | async-done | bytes 262176 | tf_op jit(solution)/shard_map/all_to_all | solution.py:68
  405.2 1.1 fusion.20
  406.2 1.1 fusion.19
  (49 shorter events, 7.2 us)
Async XLA Ops:
  0.0 272.9 %copy-start = (bf16[8,256,512]{2,1,0:T(8,128)(2,1)S(1)}, bf16[8,256,512]{2,1,0:T(8,128)(2,1)}, u32[]{:S(2)}) copy-start(bf16[8,256,512]{2,1,0:T(8,128)(2,1)} %param.13) | copy-start | bytes 6291460
  157.2 115.5 %copy-start.1 = (s32[8]{0:T(128)S(1)}, s32[8]{0:T(128)}, u32[]{:S(2)}) copy-start(s32[8]{0:T(128)} %param.15) | copy-start | bytes 100
  275.7 25.0 %all-to-all-start.2 = ((f32[1,64,2]{2,0,1:T(1,128)}), f32[1,64,2]{2,0,1:T(1,128)S(1)}, u32[]{:S(2)}, u32[]{:S(2)}) async-start(f32[1,64,2]{2,0,1:T(1,128)} %bitcast.20), calls=%async_computation.2 | async-start | bytes 65536 | tf_op jit(solution)/shard_map/all_to_all | solution.py:70
  300.7 19.2 %all-to-all-start.1 = ((f32[1,64,2]{2,0,1:T(1,128)}), f32[1,64,2]{2,0,1:T(1,128)S(1)}, u32[]{:S(2)}, u32[]{:S(2)}) async-start(f32[1,64,2]{2,0,1:T(1,128)} %bitcast.17), calls=%async_computation.1 | async-start | bytes 65536 | tf_op jit(solution)/shard_map/all_to_all | solution.py:69
  319.9 20.0 %all-to-all-start.5 = ((f32[1,64,2]{2,0,1:T(1,128)}), f32[1,64,2]{2,0,1:T(1,128)S(1)}, u32[]{:S(2)}, u32[]{:S(2)}) async-start(f32[1,64,2]{2,0,1:T(1,128)} %bitcast.38), calls=%async_computation.5 | async-start | bytes 65536 | tf_op jit(solution)/shard_map/all_to_all | solution.py:70
  339.9 18.6 %all-to-all-start.4 = ((f32[1,64,2]{2,0,1:T(1,128)}), f32[1,64,2]{2,0,1:T(1,128)S(1)}, u32[]{:S(2)}, u32[]{:S(2)}) async-start(f32[1,64,2]{2,0,1:T(1,128)} %bitcast.36), calls=%async_computation.4 | async-start | bytes 65536 | tf_op jit(solution)/shard_map/all_to_all | solution.py:69
  358.5 23.1 %all-to-all-start = ((f32[1,128,512]{2,0,1:T(1,128)}), f32[1,128,512]{2,0,1:T(1,128)S(1)}, u32[]{:S(2)}, u32[]{:S(2)}) async-start(f32[1,128,512]{2,0,1:T(1,128)} %copy.87), calls=%async_computation | async-start | bytes 524288 | tf_op jit(solution)/shard_map/all_to_all | solution.py:68
  381.6 23.2 %all-to-all-start.3 = ((f32[1,128,512]{2,0,1:T(1,128)}), f32[1,128,512]{2,0,1:T(1,128)S(1)}, u32[]{:S(2)}, u32[]{:S(2)}) async-start(f32[1,128,512]{2,0,1:T(1,128)} %copy.100), calls=%async_computation.3 | async-start | bytes 524288 | tf_op jit(solution)/shard_map/all_to_all | solution.py:68
where the time goes:
time: 409 us; the launch traced here: 408 us
  blocking collectives  261 us (64%)
  waiting for transfers between devices  76.6 us (19%)
  starting transfers between devices  45.5 us (11%)
  local copies, waits for them, and re-layouts  11.3 us (3%)
  matrix products  10.5 us (3%)
    all_gather x2, blocking collectives, attend(): lax.all_gather(pieces, 'kv', axis=3, tiled=True)  235 us
    all_to_all x2, waiting for transfers between devices, combine(): lax.all_to_all(mixture, 'kv', split_axis=1, concat_axis=1, tiled=True)  30.1 us
    all_to_all x2, waiting for transfers between devices, combine(): lax.all_to_all(totals, 'kv', split_axis=1, concat_axis=1, tiled=True)  23.4 us
    all_to_all x2, waiting for transfers between devices, combine(): lax.all_to_all(highest, 'kv', split_axis=1, concat_axis=1, tiled=True)  23.1 us
    all_to_all x2, starting transfers between devices, combine(): lax.all_to_all(totals, 'kv', split_axis=1, concat_axis=1, tiled=True)  19.6 us
    all_gather x1, blocking collectives, on_device(): lax.all_gather(new_rope, 'head', axis=2, tiled=True)  13.3 us
    all_to_all x2, starting transfers between devices, combine(): lax.all_to_all(mixture, 'kv', split_axis=1, concat_axis=1, tiled=True)  13.2 us
    all_gather x1, blocking collectives, on_device(): lax.all_gather(new_latent, 'head', axis=2, tiled=True)  12.8 us
  transfers between devices with their start and end apart: 6, of which 6 were waited for; matrix products, arithmetic and copies ran while one was open for 2% of the time, Pallas kernels for 0%

commit v1 on v0

v1 whole, which is shorter than its diff:
```python
import math

import jax
import jax.numpy as jnp
from jax import lax
from jax.experimental import pallas as pl
from jax.experimental.pallas import tpu as pltpu
from jax.sharding import PartitionSpec as P

mscale = (0.1 * math.log(40.0) + 1.0) ** 2
f32 = jnp.float32
bf16 = jnp.bfloat16
MASKED = -1e30
LOWEST = -1e29
VM = pl.BlockSpec(memory_space=pltpu.VMEM)
SM = pl.BlockSpec(memory_space=pltpu.SMEM)
MIB = 1 << 20


def queries_kernel(q_ref, uk_ref, out_ref):
    steps, requests, heads, _ = q_ref.shape
    cols = uk_ref.shape[1]
    rows = jnp.concatenate([q_ref[s, b] for b in range(requests) for s in range(steps)], axis=0)
    weights = uk_ref[...].reshape(heads * cols, uk_ref.shape[2])
    every = lax.dot_general(
        weights, rows, (((1,), (1,)), ((), ())), preferred_element_type=f32
    ).reshape(heads, cols, rows.shape[0])
    head_of = lax.broadcasted_iota(jnp.int32, every.shape[1:], 1) % heads
    own = every[0]
    for h in range(1, heads):
        own = jnp.where(head_of == h, every[h], own)
    out_ref[...] = jnp.broadcast_to(own.astype(bf16)[None], out_ref.shape)


def rotary_kernel(scale, rel_ref, qr_ref, rope_ref, lat_new_ref, rope_new_ref, lat_ref, bias_ref, keys_ref, sem):
    requests, positions, _ = lat_ref.shape
    steps = qr_ref.shape[0]
    heads = qr_ref.shape[2]
    copy = pltpu.make_async_copy(lat_ref, keys_ref, sem)
    copy.start()
    raw = lat_new_ref[...].astype(f32)
    mean = jnp.mean(raw * raw, axis=-1, keepdims=True)
    fresh = (raw * lax.rsqrt(mean + 1e-06)).astype(bf16).astype(f32)
    turned = jnp.transpose(rope_new_ref[...].astype(f32))
    place = lax.broadcasted_iota(jnp.int32, (rope_ref.shape[1], positions), 1)
    lane = lax.broadcasted_iota(jnp.int32, (steps * heads, positions), 1)
    step_of = lax.broadcasted_iota(jnp.int32, (steps * heads, positions), 0) // heads
    for b in range(requests):
        rel = rel_ref[b]
        ropes = rope_ref[b].astype(f32)
        for t in range(steps):
            n = t * requests + b
            ropes = jnp.where(place == rel + t, turned[:, n : n + 1], ropes)
        rotary = jnp.concatenate([qr_ref[s, b] for s in range(steps)], axis=0)
        score = jnp.dot(rotary, ropes.astype(bf16), preferred_element_type=f32)
        width = steps * heads
        bias_ref[b * width : (b + 1) * width, :] = jnp.where(
            lane <= rel + step_of, score * scale, MASKED
        )
    copy.wait()
    window = 16
    row = lax.broadcasted_iota(jnp.int32, (window, lat_ref.shape[2]), 0)
    for b in range(requests):
        for t in range(steps):
            at = rel_ref[b] + t
            n = t * requests + b

            @pl.when((at >= 0) & (at < positions))
            def _():
                first = pl.multiple_of((at // window) * window, window)
                old = keys_ref[b, pl.ds(first, window), :].astype(f32)
                new = jnp.where(row == at - first, fresh[n : n + 1, :], old)
                keys_ref[b, pl.ds(first, window), :] = new.astype(bf16)


def attend_kernel(scale, q_ref, keys_ref, bias_ref, uv_ref, out_ref, mix_ref, stat_ref):
    requests, positions, _ = keys_ref.shape
    heads = uv_ref.shape[0]
    items = bias_ref.shape[0]
    width = items // requests
    tile = 128
    per_tile = tile // width
    mine = lax.broadcasted_iota(jnp.int32, (positions, tile), 1) // width
    rows_of = lax.broadcasted_iota(jnp.int32, (tile, tile), 1)
    for g in range(items // tile):
        q = q_ref[:, g * tile : (g + 1) * tile]
        scores = None
        for i in range(per_tile):
            part = jnp.dot(keys_ref[g * per_tile + i], q, preferred_element_type=f32)
            scores = part if scores is None else jnp.where(mine == i, part, scores)
        turned = jnp.transpose(scores) * scale + bias_ref[g * tile : (g + 1) * tile, :]
        highest = jnp.maximum(jnp.max(turned, axis=1, keepdims=True), LOWEST)
        weights = jnp.exp(turned - highest).astype(bf16)
        totals = jnp.maximum(jnp.sum(weights.astype(f32), axis=1, keepdims=True), 1e-30)
        level = highest + jnp.log(totals)
        inverse = 1.0 / totals
        high = level.astype(bf16).astype(f32)
        rest = level - high
        middle = rest.astype(bf16).astype(f32)
        low = rest - middle
        stat_ref[g * tile : (g + 1) * tile, :] = jnp.where(
            rows_of == 0, high, jnp.where(rows_of == 1, middle, jnp.where(rows_of == 2, low, 0.0))
        )
        for i in range(per_tile):
            b = g * per_tile + i
            mix = jnp.dot(
                weights[i * width : (i + 1) * width], keys_ref[b], preferred_element_type=f32
            )
            mix = mix * inverse[i * width : (i + 1) * width]
            for c in range(mix_ref.shape[0]):
                mix_ref[c, b * width : (b + 1) * width, :] = mix[:, c * tile : (c + 1) * tile]
    each = items // heads
    upper = lax.broadcasted_iota(jnp.int32, (8, tile), 0) < 4
    for h in range(heads):
        mixed = jnp.concatenate(
            [mix_ref[c, pl.ds(h, each, stride=heads), :] for c in range(mix_ref.shape[0])], axis=1
        ).astype(bf16)
        stats = stat_ref[pl.ds(h, each, stride=heads), :]
        projected = jnp.dot(mixed, uv_ref[h], preferred_element_type=f32)
        for v in range(each // 8):
            p = projected[v * 8 : (v + 1) * 8]
            st = stats[v * 8 : (v + 1) * 8]
            first = h * (each // 4) + 2 * v
            out_ref[first] = jnp.where(upper, p, pltpu.roll(st, 4, 0)).astype(bf16)
            out_ref[first + 1] = jnp.where(upper, pltpu.roll(p, 4, 0), st).astype(bf16)


def merge_kernel(parts_ref, out_ref):
    parts = parts_ref[...].astype(f32)
    levels = jnp.sum(parts, axis=2, keepdims=True)
    factor = jnp.exp(levels - jnp.max(levels, axis=0, keepdims=True))
    values = pltpu.roll(parts, 4, 1)
    merged = jnp.sum(values * factor, axis=0) / jnp.sum(factor, axis=0)
    steps, owned, _ = out_ref.shape
    for s in range(steps):
        rows = [merged[4 + i * steps + s : 5 + i * steps + s] for i in range(owned)]
        out_ref[s] = jnp.concatenate(rows, axis=0).astype(bf16)


def exchange(array):
    return lax.all_to_all(array, "kv", split_axis=0, concat_axis=0, tiled=True)


def gather_heads(block):
    count = lax.axis_size("head")
    me = lax.axis_index("head")
    held = block[None]
    bit = 1
    while bit < count:
        other = lax.ppermute(held, "head", [(i, i ^ bit) for i in range(count)])
        upper = (me & bit) != 0
        held = jnp.concatenate(
            [jnp.where(upper, other, held), jnp.where(upper, held, other)], axis=0
        )
        bit *= 2
    return held


def absorbed(query_nope, uk_weight, shards):
    steps, requests, heads, _ = query_nope.shape
    cols = uk_weight.shape[2]
    return pl.pallas_call(
        queries_kernel,
        out_shape=jax.ShapeDtypeStruct((shards, cols, steps * requests * heads), bf16),
        in_specs=[VM, VM],
        out_specs=VM,
    )(query_nope, jnp.swapaxes(uk_weight, 1, 2))


def prepare(scale, rel, query_rope, cache_rope, lat_new, rope_new, cache_latent):
    steps, requests, heads, _ = query_rope.shape
    positions = cache_latent.shape[1]
    return pl.pallas_call(
        lambda *refs: rotary_kernel(scale, *refs),
        out_shape=(
            jax.ShapeDtypeStruct((steps * requests * heads, positions), f32),
            jax.ShapeDtypeStruct(cache_latent.shape, bf16),
        ),
        in_specs=[SM, VM, VM, VM, VM, pl.BlockSpec(memory_space=pl.ANY)],
        out_specs=(VM, VM),
        scratch_shapes=[pltpu.SemaphoreType.DMA],
        compiler_params=pltpu.CompilerParams(vmem_limit_bytes=16 * MIB),
    )(rel, query_rope, cache_rope, lat_new, rope_new, cache_latent)


def attend(scale, queries, keys, bias, uv_weight, shards):
    items = bias.shape[0]
    heads, lat, vd = uv_weight.shape
    return pl.pallas_call(
        lambda *refs: attend_kernel(scale, *refs),
        out_shape=jax.ShapeDtypeStruct((shards, 8, vd), bf16),
        in_specs=[VM] * 4,
        out_specs=VM,
        scratch_shapes=[pltpu.VMEM((lat // 128, items, 128), f32), pltpu.VMEM((items, 128), f32)],
        compiler_params=pltpu.CompilerParams(vmem_limit_bytes=24 * MIB),
    )(queries, keys, bias, uv_weight)


def merge(parts, steps, owned):
    return pl.pallas_call(
        merge_kernel,
        out_shape=jax.ShapeDtypeStruct((steps, owned, parts.shape[2]), bf16),
        in_specs=[VM],
        out_specs=VM,
    )(parts)


def on_device(
    query_nope,
    query_rope,
    new_latent,
    new_rope,
    cache_latent,
    cache_rope,
    lengths,
    uk_weight,
    uv_weight,
):
    shards = lax.axis_size("kv")
    steps, requests, heads, nope = query_nope.shape
    positions = cache_latent.shape[1]
    scale = mscale / math.sqrt(nope + query_rope.shape[3])
    columns = exchange(absorbed(query_nope, uk_weight, shards))
    queries = columns.reshape(-1, columns.shape[2])
    mine = jnp.concatenate([new_latent, new_rope], axis=2).reshape(steps * requests, -1)
    tokens = jnp.swapaxes(gather_heads(mine), 0, 1)
    width = new_latent.shape[2]
    lat_new = tokens[:, :, :width].reshape(steps * requests, -1)
    rope_new = tokens[:, :, width:].reshape(steps * requests, -1)
    rel = lengths - lax.axis_index("kv") * positions
    bias, keys = prepare(scale, rel, query_rope, cache_rope, lat_new, rope_new, cache_latent)
    parts = attend(scale, queries, keys, bias, uv_weight, shards)
    return merge(exchange(parts), steps, heads * requests // shards)


def solution(mesh):
    return jax.shard_map(
        on_device,
        mesh=mesh,
        in_specs=(
            P(None, None, "head", None),
            P(None, None, "head", None),
            P(None, None, "head"),
            P(None, None, "head"),
            P(None, "kv", None),
            P(None, None, "kv"),
            P(),
            P("head", None, "kv"),
            P("head", None, None),
        ),
        out_specs=P(None, ("head", "kv"), None),
        check_vma=False,
    )
```

time: 409 us -> 79 us (0.19)
  blocking collectives: 261 us -> 27.5 us
  waiting for transfers between devices: 76.6 us -> 5.04 us
  starting transfers between devices: 45.5 us -> 29.3 us
  matrix products: 10.5 us -> 0 us
  Pallas kernels: 0 us -> 6.58 us
  local copies, waits for them, and re-layouts: 11.3 us -> 6.68 us
    all_gather x4 -> x0, blocking collectives: 261 us -> none  [the longest x2 235 us: attend(): lax.all_gather(pieces, 'kv', axis=3, tiled=True)]
    all_to_all x6 -> x1, waiting for transfers between devices: 76.6 us -> 1.64 us  [exchange(): return lax.all_to_all(array, 'kv', split_axis=0, concat_axis=0, tiled=True)]
    all_to_all x0 -> x1, blocking collectives: none -> 27.5 us  [exchange(): return lax.all_to_all(array, 'kv', split_axis=0, concat_axis=0, tiled=True)]
    all_to_all x6 -> x1, starting transfers between devices: 45.5 us -> 18.8 us  [exchange(): return lax.all_to_all(array, 'kv', split_axis=0, concat_axis=0, tiled=True)]
    dot_general x15 -> x0, matrix products: 10.5 us -> none  [the longest x2 2.26 us: attend(): jnp.einsum('sbhr,brj->shbj', rotary, cache_rope, preferred_element_type=s...]
    ppermute x0 -> x3, starting transfers between devices: none -> 10.5 us  [gather_heads(): other = lax.ppermute(held, 'head', [(i, i ^ bit) for i in range(count)])]
    pallas_call x0 -> x4, Pallas kernels: none -> 6.58 us  [the longest x1 1.91 us: attend(): pl.pallas_call(lambda *refs: attend_kernel(scale, *refs), out_shape=jax.S...]
    unnamed x6 -> x12, local copies, waits for them, and re-layouts: 1.72 us -> 6.32 us
  transfers between devices with their start and end apart: 6 -> 4, of which waited for: 6 -> 3; matrix products, arithmetic and copies ran while one was open for 2% -> 2% of each run, Pallas kernels for 0% -> 4%
where the time goes in v1:
time: 79 us; the launch traced here: 77.6 us
  starting transfers between devices  29.3 us (37%)
  blocking collectives  27.5 us (35%)
  local copies, waits for them, and re-layouts  6.68 us (8%)
  Pallas kernels  6.58 us (8%)
  waiting for transfers between devices  5.04 us (6%)
  other arithmetic  2.42 us (3%)
    all_to_all x1, blocking collectives, exchange(): return lax.all_to_all(array, 'kv', split_axis=0, concat_axis=0, tiled=True)  27.5 us
    all_to_all x1, starting transfers between devices, exchange(): return lax.all_to_all(array, 'kv', split_axis=0, concat_axis=0, tiled=True)  18.8 us
    ppermute x3, starting transfers between devices, gather_heads(): other = lax.ppermute(held, 'head', [(i, i ^ bit) for i in range(count)])  10.5 us
    unnamed x12, local copies, waits for them, and re-layouts  6.32 us
    ppermute x3, waiting for transfers between devices, gather_heads(): other = lax.ppermute(held, 'head', [(i, i ^ bit) for i in range(count)])  3.4 us
    pallas_call x1, Pallas kernels, attend(): pl.pallas_call(lambda *refs: attend_kernel(scale, *refs), out_shape=jax.S...  1.91 us
    pallas_call x1, Pallas kernels, absorbed(): pl.pallas_call(queries_kernel, out_shape=jax.ShapeDtypeStruct((shards, co...  1.74 us
    pallas_call x1, Pallas kernels, merge(): pl.pallas_call(merge_kernel, out_shape=jax.ShapeDtypeStruct((steps, owned...  1.7 us
  transfers between devices with their start and end apart: 4, of which 3 were waited for; matrix products, arithmetic and copies ran while one was open for 2% of the time, Pallas kernels for 4%

profile of v1, /device:TPU:6, one launch (start us, length us, event | category | flops | bytes accessed | tf_op | source)
XLA Modules:
  0.0 77.6 jit_solution(3815305356551775243)
XLA Ops:
  0.0 0.0 copy-start
  0.0 0.9 %maximum_bitcast_fusion.1 = bf16[1,16,72]{2,1,0:T(8,128)(2,1)S(1)} fusion(bf16[2,8,8]{2,1,0:T(8,128)(2,1)} %param.12, bf16[2,8,64]{2,1,0:T(8,128)(2,1)} %param.11), kind=kLoop, calls=%fused_computation.7 | loop fusion | flops 4608 | bytes 4608 | tf_op jit(solution)/shard_map/broadcast_in_dim;reshape | solution.py:147
  0.9 1.9 %collective-permute-start = (bf16[1,16,72]{2,1,0:T(8,128)(2,1)S(1)}, bf16[1,16,72]{2,1,0:T(8,128)(2,1)S(1)}, u32[]{:S(2)}, u32[]{:S(2)}) collective-permute-start(bf16[1,16,72]{2,1,0:T(8,128)(2,1)S(1)} %maximum_bitcast_fusion.1), channel_id=1, source_target_pairs={{0,1},{1,0},{2,3},{3,2},{4,5},{5,4},{6,7},{7,6},{8,9},{9,8},{10,11... | collective-permute-start | bytes 6920 | tf_op jit(solution)/shard_map/ppermute | solution.py:150
  2.8 1.7 %shard_map.91 = bf16[64,8,256]{2,1,0:T(8,128)(2,1)} custom-call(bf16[2,8,16,128]{3,2,1,0:T(8,128)(2,1)} %q_ref.1, bf16[16,8,128]{2,1,0:T(8,128)(2,1)} %bitcast.13), custom_call_target="tpu_custom_call" | custom-call | tf_op jit(solution)/shard_map/pallas_call | solution.py:162
  4.6 18.8 %all-to-all-start = ((bf16[64,8,256]{2,1,0:T(8,128)(2,1)}), bf16[64,8,256]{2,1,0:T(8,128)(2,1)S(1)}, u32[]{:S(2)}, u32[]{:S(2)}) async-start(bf16[64,8,256]{2,1,0:T(8,128)(2,1)} %shard_map.91), calls=%async_computation | async-start | bytes 524288 | tf_op jit(solution)/shard_map/all_to_all | solution.py:141
  23.4 0.0 collective-permute-done
  23.4 0.8 %broadcast_select_fusion.5 = (bf16[1,16,72]{2,1,0:T(8,128)(2,1)S(1)}, bf16[1,16,72]{2,1,0:T(8,128)(2,1)S(1)}) fusion(bf16[1,16,72]{2,1,0:T(8,128)(2,1)S(1)} %collective-permute-done, pred[]{:T(512)S(6)} %ne.11, bf16[2,8,8]{2,1,0:T(8,128)(2,1)} %param.12, bf16[2,8,64]{2,1,0:T(8,128)(2,1)} %param.11), kind=kLoop, calls=%fused_computation.9 | loop fusion | flops 6912 | bytes 9217 | tf_op jit(solution)/shard_map/jit(_where)/select_n | solution.py:153
  24.2 3.5 %collective-permute-start.1 = (bf16[2,16,72]{2,1,0:T(8,128)(2,1)S(1)}, bf16[2,16,72]{2,1,0:T(8,128)(2,1)S(1)}, u32[]{:S(2)}, u32[]{:S(2)}) collective-permute-start(bf16[2,16,72]{2,1,0:T(8,128)(2,1)S(1)} %pad_maximum_fusion.1), channel_id=1, source_target_pairs={{0,2},{1,3},{2,0},{3,1},{4,6},{5,7},{6,4},{7,5},{8,10},{9,11},{10,... | collective-permute-start | bytes 13832 | tf_op jit(solution)/shard_map/ppermute | solution.py:150
  27.7 2.0 %collective-permute-done.1 = bf16[2,16,72]{2,1,0:T(8,128)(2,1)S(1)} collective-permute-done((bf16[2,16,72]{2,1,0:T(8,128)(2,1)S(1)}, bf16[2,16,72]{2,1,0:T(8,128)(2,1)S(1)}, u32[]{:S(2)}, u32[]{:S(2)}) %collective-permute-start.1) | collective-permute-done | bytes 4640 | tf_op jit(solution)/shard_map/ppermute | solution.py:150
  29.8 5.1 %collective-permute-start.2 = (bf16[4,16,72]{2,1,0:T(8,128)(2,1)S(1)}, bf16[4,16,72]{2,1,0:T(8,128)(2,1)S(1)}, u32[]{:S(2)}, u32[]{:S(2)}) collective-permute-start(bf16[4,16,72]{2,1,0:T(8,128)(2,1)S(1)} %pad_maximum_fusion), channel_id=1, source_target_pairs={{0,4},{1,5},{2,6},{3,7},{4,0},{5,1},{6,2},{7,3},{8,12},{9,13},{10,... | collective-permute-start | bytes 27656 | tf_op jit(solution)/shard_map/ppermute | solution.py:150
  34.9 0.7 broadcast_subtract_fusion.refs_0_
  35.5 1.4 %collective-permute-done.2 = bf16[4,16,72]{2,1,0:T(8,128)(2,1)S(1)} collective-permute-done((bf16[4,16,72]{2,1,0:T(8,128)(2,1)S(1)}, bf16[4,16,72]{2,1,0:T(8,128)(2,1)S(1)}, u32[]{:S(2)}, u32[]{:S(2)}) %collective-permute-start.2) | collective-permute-done | bytes 9248 | tf_op jit(solution)/shard_map/ppermute | solution.py:150
  36.9 0.1 slice.9
  37.0 0.1 reshape.10.refs_3_
  37.1 0.1 copy.19
  37.2 0.1 copy.20.refs_4_
  37.3 0.0 copy-start.3
  37.3 1.6 %copy-done.3 = bf16[8,256,512]{2,1,0:T(8,128)(2,1)S(1)} copy-done((bf16[8,256,512]{2,1,0:T(8,128)(2,1)S(1)}, bf16[8,256,512]{2,1,0:T(8,128)(2,1)}, u32[]{:S(2)}) %copy-start.3) | copy-done | bytes 2097176
  38.9 0.0 copy-start.4
  38.9 0.9 %copy-done.4 = bf16[8,64,256]{2,1,0:T(8,128)(2,1)S(1)} copy-done((bf16[8,64,256]{2,1,0:T(8,128)(2,1)S(1)}, bf16[8,64,256]{2,1,0:T(8,128)(2,1)}, u32[]{:S(2)}) %copy-start.4) | copy-done | bytes 262168
  39.9 0.0 copy-start.5
  39.9 0.8 %copy-done.5 = bf16[2,8,16,64]{3,2,1,0:T(8,128)(2,1)S(1)} copy-done((bf16[2,8,16,64]{3,2,1,0:T(8,128)(2,1)S(1)}, bf16[2,8,16,64]{3,2,1,0:T(8,128)(2,1)}, u32[]{:S(2)}) %copy-start.5) | copy-done | bytes 32792
  40.7 1.2 %shard_map.92 = (f32[256,256]{1,0:T(8,128)S(1)}, bf16[8,256,512]{2,1,0:T(8,128)(2,1)S(1)}) custom-call(s32[8]{0:T(128)S(1)} %broadcast_subtract_fusion.refs_0_, bf16[2,8,16,64]{3,2,1,0:T(8,128)(2,1)S(1)} %copy-done.5, bf16[8,64,256]{2,1,0:T(8,128)(2,1)S(1)} %copy-done.4, bf16[16,512]{1,0:T(8,128)(2,1)S(1)} %reshape.10.refs_3_, ...), custom_call_target="tpu_custom_call" | custom-call | tf_op jit(solution)/shard_map/pallas_call | solution.py:173
  41.9 0.0 copy-start.1
  41.9 1.3 %copy-done.1 = bf16[8,256,512]{2,1,0:T(8,128)(2,1)} copy-done((bf16[8,256,512]{2,1,0:T(8,128)(2,1)}, bf16[8,256,512]{2,1,0:T(8,128)(2,1)S(1)}, u32[]{:S(2)}) %copy-start.1) | copy-done | bytes 2097176
  43.3 1.6 %all-to-all-done = bf16[64,8,256]{2,1,0:T(8,128)(2,1)S(1)} async-done(((bf16[64,8,256]{2,1,0:T(8,128)(2,1)}), bf16[64,8,256]{2,1,0:T(8,128)(2,1)S(1)}, u32[]{:S(2)}, u32[]{:S(2)}) %all-to-all-start) | async-done | bytes 262176 | tf_op jit(solution)/shard_map/all_to_all | solution.py:141
  44.9 0.0 copy-done
  44.9 0.0 copy-start.2
  44.9 1.6 %copy-done.2 = bf16[8,256,512]{2,1,0:T(8,128)(2,1)S(1)} copy-done((bf16[8,256,512]{2,1,0:T(8,128)(2,1)S(1)}, bf16[8,256,512]{2,1,0:T(8,128)(2,1)}, u32[]{:S(2)}) %copy-start.2) | copy-done | bytes 2097176
  46.5 1.9 %shard_map.93 = bf16[64,8,128]{2,1,0:T(8,128)(2,1)S(1)} custom-call(bf16[512,256]{1,0:T(8,128)(2,1)S(1)} %bitcast.10, bf16[8,256,512]{2,1,0:T(8,128)(2,1)S(1)} %copy-done.2, f32[256,256]{1,0:T(8,128)S(1)} %get-tuple-element.8.refs_2_, bf16[16,512,128]{2,1,0:T(8,128)(2,1)S(1)} %copy-done), custom_call_target="tpu_custom_call" | custom-call | tf_op jit(solution)/shard_map/pallas_call | solution.py:189
  48.4 27.5 %all_to_all.10.parts_ref = bf16[64,8,128]{2,1,0:T(8,128)(2,1)} all-to-all(bf16[64,8,128]{2,1,0:T(8,128)(2,1)S(1)} %shard_map.93), channel_id=1, replica_groups=mesh['kv'=64,'head'=8] {'kv'}, dimensions={0} | all-to-all | bytes 262144 | tf_op jit(solution)/shard_map/all_to_all | solution.py:141
  75.9 1.7 %shard_map.94 = bf16[2,2,128]{2,1,0:T(2,128)(2,1)} custom-call(bf16[64,8,128]{2,1,0:T(8,128)(2,1)} %all_to_all.10.parts_ref), custom_call_target="tpu_custom_call" | custom-call | tf_op jit(solution)/shard_map/pallas_call | solution.py:200
  (6 shorter events, 0.1 us)
Async XLA Ops:
  0.0 44.9 %copy-start = (bf16[16,512,128]{2,1,0:T(8,128)(2,1)S(1)}, bf16[16,512,128]{2,1,0:T(8,128)(2,1)}, u32[]{:S(2)}) copy-start(bf16[16,512,128]{2,1,0:T(8,128)(2,1)} %refs_3_.1) | copy-start | bytes 6291460
  0.9 22.5 %collective-permute-start = (bf16[1,16,72]{2,1,0:T(8,128)(2,1)S(1)}, bf16[1,16,72]{2,1,0:T(8,128)(2,1)S(1)}, u32[]{:S(2)}, u32[]{:S(2)}) collective-permute-start(bf16[1,16,72]{2,1,0:T(8,128)(2,1)S(1)} %maximum_bitcast_fusion.1), channel_id=1, source_target_pairs={{0,1},{1,0},{2,3},{3,2},{4,5},{5,4},{6,7},{7,6},{8,9},{9,8},{10,11... | collective-permute-start | bytes 6920 | tf_op jit(solution)/shard_map/ppermute | solution.py:150
  4.6 40.3 %all-to-all-start = ((bf16[64,8,256]{2,1,0:T(8,128)(2,1)}), bf16[64,8,256]{2,1,0:T(8,128)(2,1)S(1)}, u32[]{:S(2)}, u32[]{:S(2)}) async-start(bf16[64,8,256]{2,1,0:T(8,128)(2,1)} %shard_map.91), calls=%async_computation | async-start | bytes 524288 | tf_op jit(solution)/shard_map/all_to_all | solution.py:141
  24.2 5.5 %collective-permute-start.1 = (bf16[2,16,72]{2,1,0:T(8,128)(2,1)S(1)}, bf16[2,16,72]{2,1,0:T(8,128)(2,1)S(1)}, u32[]{:S(2)}, u32[]{:S(2)}) collective-permute-start(bf16[2,16,72]{2,1,0:T(8,128)(2,1)S(1)} %pad_maximum_fusion.1), channel_id=1, source_target_pairs={{0,2},{1,3},{2,0},{3,1},{4,6},{5,7},{6,4},{7,5},{8,10},{9,11},{10,... | collective-permute-start | bytes 13832 | tf_op jit(solution)/shard_map/ppermute | solution.py:150
  29.8 7.1 %collective-permute-start.2 = (bf16[4,16,72]{2,1,0:T(8,128)(2,1)S(1)}, bf16[4,16,72]{2,1,0:T(8,128)(2,1)S(1)}, u32[]{:S(2)}, u32[]{:S(2)}) collective-permute-start(bf16[4,16,72]{2,1,0:T(8,128)(2,1)S(1)} %pad_maximum_fusion), channel_id=1, source_target_pairs={{0,4},{1,5},{2,6},{3,7},{4,0},{5,1},{6,2},{7,3},{8,12},{9,13},{10,... | collective-permute-start | bytes 27656 | tf_op jit(solution)/shard_map/ppermute | solution.py:150
  37.3 1.6 %copy-start.3 = (bf16[8,256,512]{2,1,0:T(8,128)(2,1)S(1)}, bf16[8,256,512]{2,1,0:T(8,128)(2,1)}, u32[]{:S(2)}) copy-start(bf16[8,256,512]{2,1,0:T(8,128)(2,1)} %refs_5_.1) | copy-start | bytes 6291460
  38.9 0.9 %copy-start.4 = (bf16[8,64,256]{2,1,0:T(8,128)(2,1)S(1)}, bf16[8,64,256]{2,1,0:T(8,128)(2,1)}, u32[]{:S(2)}) copy-start(bf16[8,64,256]{2,1,0:T(8,128)(2,1)} %refs_2_.1) | copy-start | bytes 786436
  39.9 0.8 %copy-start.5 = (bf16[2,8,16,64]{3,2,1,0:T(8,128)(2,1)S(1)}, bf16[2,8,16,64]{3,2,1,0:T(8,128)(2,1)}, u32[]{:S(2)}) copy-start(bf16[2,8,16,64]{3,2,1,0:T(8,128)(2,1)} %refs_1_.1) | copy-start | bytes 98308
  41.9 1.3 %copy-start.1 = (bf16[8,256,512]{2,1,0:T(8,128)(2,1)}, bf16[8,256,512]{2,1,0:T(8,128)(2,1)S(1)}, u32[]{:S(2)}) copy-start(bf16[8,256,512]{2,1,0:T(8,128)(2,1)S(1)} %get-tuple-element.7.refs_1_) | copy-start | bytes 6291460
  44.9 1.6 %copy-start.2 = (bf16[8,256,512]{2,1,0:T(8,128)(2,1)S(1)}, bf16[8,256,512]{2,1,0:T(8,128)(2,1)}, u32[]{:S(2)}) copy-start(bf16[8,256,512]{2,1,0:T(8,128)(2,1)} %copy-done.1) | copy-start | bytes 6291460

commit v2 on v1

v2 whole, which is shorter than its diff:
```python
import math

import jax
import jax.numpy as jnp
from jax import lax
from jax.experimental import pallas as pl
from jax.experimental.pallas import tpu as pltpu
from jax.sharding import PartitionSpec as P

mscale = (0.1 * math.log(40.0) + 1.0) ** 2
f32 = jnp.float32
bf16 = jnp.bfloat16
MASKED = -1e30
LOWEST = -1e29
VM = pl.BlockSpec(memory_space=pltpu.VMEM)
SM = pl.BlockSpec(memory_space=pltpu.SMEM)
HBM = pl.BlockSpec(memory_space=pltpu.HBM)
RINGS = 4
ALONG, ACROSS, ALL = 10, 2, 42


def fetch(*copies):
    copies = [pltpu.make_async_copy(*copy) for copy in copies]
    for copy in copies:
        copy.start()
    for copy in copies:
        copy.wait()


def queries_kernel(q_hbm, uk_hbm, out_ref, q_ref, uk_ref, sems):
    fetch((uk_hbm, uk_ref, sems.at[0]), (q_hbm, q_ref, sems.at[1]))
    steps, requests, heads, _ = q_ref.shape
    cols = uk_ref.shape[1]
    rows = jnp.concatenate([q_ref[s, b] for b in range(requests) for s in range(steps)], axis=0)
    weights = uk_ref[...].reshape(heads * cols, uk_ref.shape[2])
    every = lax.dot_general(
        weights, rows, (((1,), (1,)), ((), ())), preferred_element_type=f32
    ).reshape(heads, cols, rows.shape[0])
    head_of = lax.broadcasted_iota(jnp.int32, every.shape[1:], 1) % heads
    own = every[0]
    for h in range(1, heads):
        own = jnp.where(head_of == h, every[h], own)
    out_ref[...] = jnp.broadcast_to(own.astype(bf16)[None], out_ref.shape)


def repeat_kernel(shift, in_ref, *refs):
    out_ref = refs[-1]
    count, cols, items = in_ref.shape
    rows = in_ref[...].reshape(count * cols, items)
    first = (count - shift) * cols
    ordered = jnp.concatenate([rows[first:], rows[:first]], axis=0)
    out_ref[...] = jnp.broadcast_to(ordered[None], out_ref.shape)


def tokens_kernel(lat_hbm, rope_hbm, _, out_ref, lat_ref, rope_ref, sems):
    fetch((lat_hbm, lat_ref, sems.at[0]), (rope_hbm, rope_ref, sems.at[1]))
    steps, requests, lat = lat_ref.shape
    rope = rope_ref.shape[2]
    rows = steps * requests

    def one_hot(shape, shift):
        return (
            lax.broadcasted_iota(jnp.int32, shape, 1) == lax.broadcasted_iota(jnp.int32, shape, 0) + shift
        ).astype(bf16)

    def joined(ref):
        return jnp.concatenate([ref[t] for t in range(steps)], axis=0)

    placed = jnp.dot(joined(lat_ref), one_hot((lat, 128), 64), preferred_element_type=f32)
    placed += jnp.dot(joined(rope_ref), one_hot((rope, 128), 8), preferred_element_type=f32)
    to = lax.broadcasted_iota(jnp.int32, (rows, rows), 0)
    source = lax.broadcasted_iota(jnp.int32, (rows, rows), 1)
    order = ((to % steps) * requests + to // steps == source).astype(bf16)
    out_ref[...] = jnp.dot(order, placed.astype(bf16), preferred_element_type=f32).astype(bf16)


def own_rows(shard, items, requests, heads, steps):
    row = lax.broadcasted_iota(jnp.int32, (8, items), 0) - 4
    item = lax.broadcasted_iota(jnp.int32, (8, items), 1)
    owned = 4 // steps
    groups = requests // owned
    request = owned * (shard % groups) + row // steps
    wanted = request * (steps * heads) + (row % steps) * heads + shard // groups
    return ((row >= 0) & (item == wanted)).astype(bf16)


def prepare_kernel(
    scale, place_ref, length_ref, qr_hbm, rope_hbm, keys_hbm, uv_hbm, _,
    bias_ref, own_ref, keys_ref, uv_own_ref, qr_ref, rope_ref, sems,
):
    steps, requests, heads, ropes = qr_ref.shape
    shard = place_ref[0]
    owner = shard // (requests // (4 // steps))
    pairs = [
        (rope_hbm, rope_ref), (qr_hbm, qr_ref), (keys_hbm, keys_ref), (uv_hbm.at[owner], uv_own_ref),
    ]
    copies = [pltpu.make_async_copy(p, q, sems.at[i]) for i, (p, q) in enumerate(pairs)]
    for copy in copies:
        copy.start()
    copies[0].wait()
    copies[1].wait()
    positions = rope_ref.shape[2]
    width = steps * heads
    lane = lax.broadcasted_iota(jnp.int32, (width, positions), 1) + shard * positions
    rows = [
        jnp.concatenate([qr_ref[s, b] for s in range(steps)], axis=0) for b in range(requests)
    ]
    for b in range(requests):
        score = jnp.dot(rows[b], rope_ref[b], preferred_element_type=f32)
        bias_ref[b * width : (b + 1) * width, :] = jnp.where(
            lane < length_ref[b], score * scale, MASKED
        )
    every = jnp.concatenate(rows, axis=0)
    own = own_rows(shard, width * requests, requests, heads, steps)
    mine = jnp.dot(own, every, preferred_element_type=f32).astype(bf16)
    groups = own_ref.shape[0]
    each = ropes // groups
    at = lax.broadcasted_iota(jnp.int32, (ropes, 128), 0)
    to = lax.broadcasted_iota(jnp.int32, (ropes, 128), 1)
    for g in range(groups):
        spread = (at == to - 8 + each * g) & (to >= 8) & (to < 8 + each)
        own_ref[g] = jnp.dot(mine, spread.astype(bf16), preferred_element_type=f32)
    for copy in copies[2:]:
        copy.wait()


def attend_kernel(
    scale, turn, shift, place_ref, q_ref, keys_ref, bias_ref, uv_hbm, token_ref,
    out_ref, own_ref, mix_ref, stat_ref, uv_ref, sem,
):
    copy = pltpu.make_async_copy(uv_hbm, uv_ref, sem)
    copy.start()
    requests, positions, _ = keys_ref.shape
    heads = uv_ref.shape[0]
    items = bias_ref.shape[0]
    width = items // requests
    tile = 128
    per_tile = tile // width
    mine = lax.broadcasted_iota(jnp.int32, (positions, tile), 1) // width
    rows_of = lax.broadcasted_iota(jnp.int32, (tile, tile), 1)
    rings = q_ref.shape[0]
    queries = jnp.concatenate([q_ref[(i - turn) % rings] for i in range(rings)], axis=0)
    for g in range(items // tile):
        q = queries[:, g * tile : (g + 1) * tile]
        scores = None
        for i in range(per_tile):
            part = jnp.dot(keys_ref[g * per_tile + i], q, preferred_element_type=f32)
            scores = part if scores is None else jnp.where(mine == i, part, scores)
        turned = jnp.transpose(scores) * scale + bias_ref[g * tile : (g + 1) * tile, :]
        highest = jnp.maximum(jnp.max(turned, axis=1, keepdims=True), LOWEST)
        weights = jnp.exp(turned - highest).astype(bf16)
        totals = jnp.maximum(jnp.sum(weights.astype(f32), axis=1, keepdims=True), 1e-30)
        level = highest + jnp.log(totals)
        inverse = 1.0 / totals
        high = level.astype(bf16).astype(f32)
        rest = level - high
        middle = rest.astype(bf16).astype(f32)
        low = rest - middle
        stat_ref[g * tile : (g + 1) * tile, :] = jnp.where(
            rows_of == 0, high, jnp.where(rows_of == 1, middle, jnp.where(rows_of == 2, low, 0.0))
        )
        for i in range(per_tile):
            b = g * per_tile + i
            mix = jnp.dot(
                weights[i * width : (i + 1) * width], keys_ref[b], preferred_element_type=f32
            )
            mix = mix * inverse[i * width : (i + 1) * width]
            for c in range(mix_ref.shape[0]):
                mix_ref[c, b * width : (b + 1) * width, :] = mix[:, c * tile : (c + 1) * tile]
    each = items // heads
    own = own_rows(place_ref[0], items, requests, heads, width // heads)
    own_ref[...] = lax.dot_general(
        own, queries, (((1,), (1,)), ((), ())), preferred_element_type=f32
    )
    token = token_ref[...].astype(f32)
    copy.wait()
    upper = lax.broadcasted_iota(jnp.int32, (8, tile), 0) < 4
    for h in range(heads):
        mixed = jnp.concatenate(
            [mix_ref[c, pl.ds(h, each, stride=heads), :] for c in range(mix_ref.shape[0])], axis=1
        ).astype(bf16)
        stats = stat_ref[pl.ds(h, each, stride=heads), :] + token
        projected = jnp.dot(mixed, uv_ref[h], preferred_element_type=f32)
        for v in range(each // 8):
            p = projected[v * 8 : (v + 1) * 8]
            st = stats[v * 8 : (v + 1) * 8]
            first = h * (each // 4) + 2 * v
            shards = out_ref.shape[0]
            out_ref[(first - shift) % shards] = jnp.where(upper, p, pltpu.roll(st, 4, 0)).astype(bf16)
            out_ref[(first + 1 - shift) % shards] = jnp.where(upper, pltpu.roll(p, 4, 0), st).astype(bf16)


def merge_kernel(scale, shift, place_ref, parts_ref, q_ref, rope_ref, uv_ref, out_ref):
    steps, owned, _ = out_ref.shape
    groups = rope_ref.shape[0]
    parts = parts_ref[...].astype(f32)
    lanes = lax.broadcasted_iota(jnp.int32, parts.shape, 2)
    levels = jnp.sum(jnp.where(lanes < 3, parts, 0.0), axis=2, keepdims=True)
    lane = lanes[0]
    row = lax.broadcasted_iota(jnp.int32, (8, 1), 0)
    blocks = [
        parts_ref[(g + groups - place_ref[1]) % groups + parts.shape[0] - shift].astype(f32)
        for g in range(groups)
    ]
    raw = jnp.concatenate(
        [
            jnp.where(lane < 64, pltpu.roll(blocks[g], 64, 1), blocks[g + 1])
            for g in range(0, groups, 2)
        ],
        axis=1,
    )
    mean = jnp.mean(raw * raw, axis=1, keepdims=True)
    key = (raw * lax.rsqrt(mean + 1e-06)).astype(bf16)
    value = jnp.dot(key, uv_ref[...], preferred_element_type=f32)
    key = key.astype(f32)
    queries = q_ref[...]

    def score(back):
        ropes = sum(pltpu.roll(blocks[g], back, 0) * rope_ref[g] for g in range(groups))
        latent = jnp.sum(pltpu.roll(key, back, 0) * queries, axis=1, keepdims=True)
        return (latent + jnp.sum(ropes, axis=1, keepdims=True)) * scale

    summit = jnp.max(levels, axis=0)
    fresh = []
    for back in range(steps):
        level = jnp.where(row % steps >= back, score(back), MASKED)
        fresh.append((level, pltpu.roll(value, back, 0)))
        summit = jnp.maximum(summit, level)
    factor = jnp.exp(levels - summit[None])
    merged = jnp.sum(pltpu.roll(parts, 4, 1) * factor, axis=0)
    totals = jnp.sum(factor, axis=0)
    for level, values in fresh:
        factor = jnp.exp(level - summit)
        merged += factor * values
        totals += factor
    merged = merged / totals
    for s in range(steps):
        rows = [merged[4 + i * steps + s : 5 + i * steps + s] for i in range(owned)]
        out_ref[s] = jnp.concatenate(rows, axis=0).astype(bf16)


def exchange(array, groups):
    return lax.all_to_all(
        array, "kv", split_axis=0, concat_axis=0, tiled=True, axis_index_groups=groups
    )


def spread_tokens(block):
    shards, groups = lax.axis_size("kv"), lax.axis_size("head")
    pairs = [
        (k * groups + (g + k) % groups, k * groups + g) for k in range(shards) for g in range(groups)
    ]
    return lax.ppermute(block, ("kv", "head"), pairs)


def near(shape, kind):
    return pltpu.VMEM(shape, kind)


def pinned(space, *arrays):
    return [pltpu.with_memory_space_constraint(array, space) for array in arrays]


def limit(mib):
    return pltpu.CompilerParams(vmem_limit_bytes=mib << 20)


def cost(flops, moved):
    return pl.CostEstimate(flops=flops, bytes_accessed=moved, transcendentals=0)


def absorbed(query_nope, uk_weight, copies):
    steps, requests, heads, _ = query_nope.shape
    uk = jnp.swapaxes(uk_weight, 1, 2)
    return pl.pallas_call(
        queries_kernel,
        out_shape=jax.ShapeDtypeStruct((copies, uk.shape[1], steps * requests * heads), bf16),
        in_specs=[HBM, HBM],
        out_specs=VM,
        scratch_shapes=[
            pltpu.VMEM(query_nope.shape, bf16),
            pltpu.VMEM(uk.shape, bf16),
            pltpu.SemaphoreType.DMA((2,)),
        ],
        compiler_params=limit(4),
    )(*pinned(pltpu.HBM, query_nope, uk))


def repeated(columns, shift, copies, *after):
    count, cols, items = columns.shape
    return pl.pallas_call(
        lambda *refs: repeat_kernel(shift, *refs),
        out_shape=jax.ShapeDtypeStruct((copies, count * cols, items), bf16),
        in_specs=[VM] + [pl.BlockSpec(memory_space=pl.ANY)] * len(after),
        out_specs=VM,
        compiler_params=limit(4),
    )(columns, *after)


def tokens(new_latent, new_rope, after):
    rows = new_latent.shape[0] * new_latent.shape[1]
    return pl.pallas_call(
        tokens_kernel,
        out_shape=jax.ShapeDtypeStruct((rows, 128), bf16),
        in_specs=[HBM, HBM, pl.BlockSpec(memory_space=pl.ANY)],
        out_specs=VM,
        scratch_shapes=[
            pltpu.VMEM(new_latent.shape, bf16),
            pltpu.VMEM(new_rope.shape, bf16),
            pltpu.SemaphoreType.DMA((2,)),
        ],
        compiler_params=limit(4),
        cost_estimate=cost(1 << 20, 1 << 16),
    )(*pinned(pltpu.HBM, new_latent, new_rope), after)


def prepare(scale, place, lengths, query_rope, cache_rope, cache_latent, uv_weight, after, groups):
    steps, requests, heads, _ = query_rope.shape
    positions = cache_rope.shape[2]
    return pl.pallas_call(
        lambda *refs: prepare_kernel(scale, *refs),
        out_shape=(
            near((steps * requests * heads, positions), f32),
            near((groups, 8, 128), f32),
            near(cache_latent.shape, bf16),
            near(uv_weight.shape[1:], bf16),
        ),
        in_specs=[SM, SM] + [HBM] * 4 + [pl.BlockSpec(memory_space=pl.ANY)],
        out_specs=(VM,) * 4,
        scratch_shapes=[
            pltpu.VMEM(query_rope.shape, bf16),
            pltpu.VMEM(cache_rope.shape, bf16),
            pltpu.SemaphoreType.DMA((4,)),
        ],
        compiler_params=limit(16),
        cost_estimate=cost(1 << 28, 1 << 22),
    )(
        place,
        lengths,
        *pinned(pltpu.HBM, query_rope, cache_rope, cache_latent, uv_weight),
        after,
    )


def attend(scale, turn, shift, place, queries, keys, bias, uv_weight, token, shards):
    items = bias.shape[0]
    heads, lat, vd = uv_weight.shape
    return pl.pallas_call(
        lambda *refs: attend_kernel(scale, turn, shift, *refs),
        out_shape=(
            jax.ShapeDtypeStruct((shards, 8, vd), bf16),
            jax.ShapeDtypeStruct((8, lat), f32),
        ),
        in_specs=[SM, VM, VM, VM, HBM, VM],
        out_specs=(VM, VM),
        scratch_shapes=[
            pltpu.VMEM((lat // 128, items, 128), f32),
            pltpu.VMEM((items, 128), f32),
            pltpu.VMEM(uv_weight.shape, bf16),
            pltpu.SemaphoreType.DMA,
        ],
        compiler_params=limit(16),
    )(place, queries, *pinned(pltpu.VMEM, keys, bias), *pinned(pltpu.HBM, uv_weight), token)


def merge(scale, shift, place, parts, queries, ropes, uv_own, steps, owned):
    return pl.pallas_call(
        lambda *refs: merge_kernel(scale, shift, *refs),
        out_shape=jax.ShapeDtypeStruct((steps, owned, parts.shape[2]), bf16),
        in_specs=[SM] + [VM] * 4,
        out_specs=VM,
        compiler_params=limit(8),
    )(place, parts, queries, ropes, uv_own)


def on_device(
    query_nope,
    query_rope,
    new_latent,
    new_rope,
    cache_latent,
    cache_rope,
    lengths,
    uk_weight,
    uv_weight,
):
    shards, groups = lax.axis_size("kv"), lax.axis_size("head")
    steps, requests, heads, nope = query_nope.shape
    owned = heads * requests // shards
    scale = mscale / math.sqrt(nope + query_rope.shape[3])
    place = jnp.stack([lax.axis_index("kv"), lax.axis_index("head")]).astype(jnp.int32)
    rings = RINGS
    size = shards // rings
    along = [[r * size + (i + ALONG) % size for i in range(size)] for r in range(rings)]
    across = [[(i + ACROSS) % rings * size + p for i in range(rings)] for p in range(size)]
    everyone = [[(i + ALL) % shards for i in range(shards)]]
    block = absorbed(query_nope, uk_weight, size)
    ring = exchange(block, along)
    token = spread_tokens(tokens(new_latent, new_rope, block))
    bias, ropes, keys, uv_own = prepare(
        scale, place, lengths, query_rope, cache_rope, cache_latent, uv_weight, block, groups
    )
    queries = exchange(repeated(ring, ALONG, rings, ropes, token), across)
    parts, own = attend(scale, ACROSS, ALL, place, queries, keys, bias, uv_weight, token, shards)
    parts = exchange(parts, everyone)
    return merge(scale, ALL, place, parts, own, ropes, uv_own, steps, owned)


def solution(mesh):
    return jax.shard_map(
        on_device,
        mesh=mesh,
        in_specs=(
            P(None, None, "head", None),
            P(None, None, "head", None),
            P(None, None, "head"),
            P(None, None, "head"),
            P(None, "kv", None),
            P(None, None, "kv"),
            P(),
            P("head", None, "kv"),
            P("head", None, None),
        ),
        out_specs=P(None, ("head", "kv"), None),
        check_vma=False,
    )
```

time: 79 us -> 65 us (0.82)
  starting transfers between devices: 29.3 us -> 17.7 us
  blocking collectives: 27.5 us -> 35.6 us
  local copies, waits for them, and re-layouts: 6.68 us -> 0.66 us
  waiting for transfers between devices: 5.04 us -> 0.77 us
  Pallas kernels: 6.58 us -> 9.08 us
  other arithmetic: 2.42 us -> 0.08 us
    ppermute x3 -> x1, starting transfers between devices: 10.5 us -> 0.66 us  [spread_tokens(): return lax.ppermute(block, ('kv', 'head'), pairs)]
    all_to_all x1 -> x2, blocking collectives: 27.5 us -> 35.6 us  [exchange(): lax.all_to_all(array, 'kv', split_axis=0, concat_axis=0, tiled=True, axis...]
    unnamed x12 -> x2, local copies, waits for them, and re-layouts: 6.32 us -> 0.66 us
    ppermute x3 -> x1, waiting for transfers between devices: 3.4 us -> 0.01 us  [spread_tokens(): return lax.ppermute(block, ('kv', 'head'), pairs)]
    pallas_call x4 -> x6, Pallas kernels: 6.58 us -> 9.08 us  [the longest x1 2.66 us: attend(): pl.pallas_call(lambda *refs: attend_kernel(scale, turn, shift, *refs), ou...]
    all_to_all x1, starting transfers between devices: 18.8 us -> 17.1 us  [exchange(): lax.all_to_all(array, 'kv', split_axis=0, concat_axis=0, tiled=True, axis...]
    all_to_all x1, waiting for transfers between devices: 1.64 us -> 0.77 us  [exchange(): lax.all_to_all(array, 'kv', split_axis=0, concat_axis=0, tiled=True, axis...]
    another operation x1, other arithmetic: 0.93 us -> 0.08 us  [on_device(): jnp.stack([lax.axis_index('kv'), lax.axis_index('head')]).astype(jnp.int32)]
  transfers between devices with their start and end apart: 4 -> 2, of which waited for: 3 -> 1; matrix products, arithmetic and copies ran while one was open for 2% -> 0% of each run, Pallas kernels for 4% -> 5%
where the time goes in v2:
time: 65 us; the launch traced here: 64 us
  blocking collectives  35.6 us (55%)
  starting transfers between devices  17.7 us (27%)
  Pallas kernels  9.08 us (14%)
  waiting for transfers between devices  0.77 us (1%)
  local copies, waits for them, and re-layouts  0.66 us (1%)
    all_to_all x2, blocking collectives, exchange(): lax.all_to_all(array, 'kv', split_axis=0, concat_axis=0, tiled=True, axis...  35.6 us
    all_to_all x1, starting transfers between devices, exchange(): lax.all_to_all(array, 'kv', split_axis=0, concat_axis=0, tiled=True, axis...  17.1 us
    pallas_call x1, Pallas kernels, attend(): pl.pallas_call(lambda *refs: attend_kernel(scale, turn, shift, *refs), ou...  2.66 us
    pallas_call x1, Pallas kernels, prepare(): pl.pallas_call(lambda *refs: prepare_kernel(scale, *refs), out_shape=(nea...  2.31 us
    pallas_call x1, Pallas kernels, absorbed(): pl.pallas_call(queries_kernel, out_shape=jax.ShapeDtypeStruct((copies, uk...  1.66 us
    pallas_call x1, Pallas kernels, merge(): pl.pallas_call(lambda *refs: merge_kernel(scale, shift, *refs), out_shape...  1.47 us
  transfers between devices with their start and end apart: 2, of which 1 were waited for; matrix products, arithmetic and copies ran while one was open for 0% of the time, Pallas kernels for 5%

profile of v2, /device:TPU:6, one launch (start us, length us, event | category | flops | bytes accessed | tf_op | source)
XLA Modules:
  0.0 64.0 jit_solution(2245044254205937421)
XLA Ops:
  0.0 1.7 %shard_map.91.refs_6_._ = bf16[16,8,256]{2,1,0:T(8,128)(2,1)} custom-call(bf16[2,8,16,128]{3,2,1,0:T(8,128)(2,1)} %q_hbm.1, bf16[16,8,128]{2,1,0:T(8,128)(2,1)} %bitcast.3), custom_call_target="tpu_custom_call" | custom-call | tf_op jit(solution)/shard_map/pallas_call | solution.py:275
  1.7 17.1 %all-to-all-start = ((bf16[16,8,256]{2,1,0:T(8,128)(2,1)}), bf16[16,8,256]{2,1,0:T(8,128)(2,1)S(1)}, u32[]{:S(2)}, u32[]{:S(2)}) async-start(bf16[16,8,256]{2,1,0:T(8,128)(2,1)} %shard_map.91.refs_6_._), calls=%async_computation | async-start | bytes 131072 | tf_op jit(solution)/shard_map/all_to_all | solution.py:243
  18.7 1.0 %shard_map.93 = bf16[16,128]{1,0:T(8,128)(2,1)S(1)} custom-call(bf16[2,8,64]{2,1,0:T(8,128)(2,1)} %lat_hbm.1, bf16[2,8,8]{2,1,0:T(8,128)(2,1)} %rope_hbm.1, bf16[16,8,256]{2,1,0:T(8,128)(2,1)} %shard_map.91.refs_6_._), custom_call_target="tpu_custom_call" | custom-call | flops 1048576 | bytes 65536 | tf_op jit(solution)/shard_map/pallas_call | solution.py:302
  19.7 0.7 %collective-permute-start = (bf16[16,128]{1,0:T(8,128)(2,1)S(1)}, bf16[16,128]{1,0:T(8,128)(2,1)S(1)}, u32[]{:S(2)}, u32[]{:S(2)}) collective-permute-start(bf16[16,128]{1,0:T(8,128)(2,1)S(1)} %shard_map.93), channel_id=1, source_target_pairs={{0,0},{1,1},{2,2},{3,3},{4,4},{5,5},{6,6},{7,7},{9,8},{10,9},{11,1... | collective-permute-start | bytes 12296 | tf_op jit(solution)/shard_map/ppermute | solution.py:253
  20.4 0.1 pad_add_fusion.refs_0_
  20.5 0.0 copy-start
  20.5 0.7 %copy-done = s32[8]{0:T(128)S(1)} copy-done((s32[8]{0:T(128)S(1)}, s32[8]{0:T(128)}, u32[]{:S(2)}) %copy-start) | copy-done | bytes 56
  21.1 2.3 %shard_map.92 = (f32[256,256]{1,0:T(8,128)S(1)}, f32[8,8,128]{2,1,0:T(8,128)S(1)}, bf16[8,256,512]{2,1,0:T(8,128)(2,1)S(1)}, bf16[512,128]{1,0:T(8,128)(2,1)S(1)}) custom-call(s32[2]{0:T(128)S(1)} %pad_add_fusion.refs_0_, s32[8]{0:T(128)S(1)} %copy-done, bf16[2,8,16,64]{3,2,1,0:T(8,128)(2,1)} %refs_2_.1, bf16[8,64,256]{2,1,0:T(8,128)(2,1)} %refs_3_.1, ...), custom_call_target="tpu_custom_call" | custom-call | flops 268435456 | bytes 4194304 | tf_op jit(solution)/shard_map/pallas_call | solution.py:320
  23.4 0.0 collective-permute-done.refs_2_.refs_5_
  23.4 0.8 %all-to-all-done.refs_0_ = bf16[16,8,256]{2,1,0:T(8,128)(2,1)S(1)} async-done(((bf16[16,8,256]{2,1,0:T(8,128)(2,1)}), bf16[16,8,256]{2,1,0:T(8,128)(2,1)S(1)}, u32[]{:S(2)}, u32[]{:S(2)}) %all-to-all-start) | async-done | bytes 65568 | tf_op jit(solution)/shard_map/all_to_all | solution.py:243
  24.2 8.8 %all_to_all.15.refs_1_ = bf16[4,128,256]{2,1,0:T(8,128)(2,1)S(1)} all-to-all(bf16[4,128,256]{2,1,0:T(8,128)(2,1)S(1)} %shard_map.94), channel_id=1, replica_groups={{256,384,0,128},{264,392,8,136},{272,400,16,144},{280,408,24,152},{288,..., dimensions={0} | all-to-all | bytes 524288 | tf_op jit(solution)/shard_map/all_to_all | solution.py:243
  33.0 2.7 %shard_map.95 = (bf16[64,8,128]{2,1,0:T(8,128)(2,1)S(1)}, f32[8,512]{1,0:T(8,128)S(1)}) custom-call(s32[2]{0:T(128)S(1)} %pad_add_fusion.refs_0_, bf16[4,128,256]{2,1,0:T(8,128)(2,1)S(1)} %all_to_all.15.refs_1_, bf16[8,256,512]{2,1,0:T(8,128)(2,1)S(1)} %get-tuple-element.12.refs_2_, f32[256,256]{1,0:T(8,128)S(1)} %get-tuple-element.13.refs_3_, ...), custom_call_target="tpu_custom_call" | custom-call | tf_op jit(solution)/shard_map/pallas_call | solution.py:348
  35.7 26.9 %all_to_all.16.refs_1_ = bf16[64,8,128]{2,1,0:T(8,128)(2,1)S(1)} all-to-all(bf16[64,8,128]{2,1,0:T(8,128)(2,1)S(1)} %get-tuple-element.14), channel_id=1, replica_groups={{336,344,352,360,368,376,384,392,400,408,416,424,432,440,448,456,464,47..., dimensions={0} | all-to-all | bytes 262144 | tf_op jit(solution)/shard_map/all_to_all | solution.py:243
  62.5 1.5 %shard_map.96 = bf16[2,2,128]{2,1,0:T(2,128)(2,1)} custom-call(s32[2]{0:T(128)S(1)} %pad_add_fusion.refs_0_, bf16[64,8,128]{2,1,0:T(8,128)(2,1)S(1)} %all_to_all.16.refs_1_, f32[8,512]{1,0:T(8,128)S(1)} %get-tuple-element.15.refs_2_, f32[8,8,128]{2,1,0:T(8,128)S(1)} %get-tuple-element.11.refs_1_.refs_3_, bf16[512,128]{1,0:T(8,128)(2,1)S(1)} %get-tuple-element.16.refs_4_), custom_call_target="tpu_custom_call" | custom-call | tf_op jit(solution)/shard_map/pallas_call | solution.py:367
  (1 shorter events, 0.0 us)
Async XLA Ops:
  1.7 22.5 %all-to-all-start = ((bf16[16,8,256]{2,1,0:T(8,128)(2,1)}), bf16[16,8,256]{2,1,0:T(8,128)(2,1)S(1)}, u32[]{:S(2)}, u32[]{:S(2)}) async-start(bf16[16,8,256]{2,1,0:T(8,128)(2,1)} %shard_map.91.refs_6_._), calls=%async_computation | async-start | bytes 131072 | tf_op jit(solution)/shard_map/all_to_all | solution.py:243
  19.7 3.7 %collective-permute-start = (bf16[16,128]{1,0:T(8,128)(2,1)S(1)}, bf16[16,128]{1,0:T(8,128)(2,1)S(1)}, u32[]{:S(2)}, u32[]{:S(2)}) collective-permute-start(bf16[16,128]{1,0:T(8,128)(2,1)S(1)} %shard_map.93), channel_id=1, source_target_pairs={{0,0},{1,1},{2,2},{3,3},{4,4},{5,5},{6,6},{7,7},{9,8},{10,9},{11,1... | collective-permute-start | bytes 12296 | tf_op jit(solution)/shard_map/ppermute | solution.py:253
  20.5 0.7 %copy-start = (s32[8]{0:T(128)S(1)}, s32[8]{0:T(128)}, u32[]{:S(2)}) copy-start(s32[8]{0:T(128)} %refs_1_.1) | copy-start | bytes 100

commit v3 on v2

--- a/solution.py
+++ b/solution.py
@@ -16,7 +16,7 @@
 SM = pl.BlockSpec(memory_space=pltpu.SMEM)
 HBM = pl.BlockSpec(memory_space=pltpu.HBM)
 RINGS = 4
-ALONG, ACROSS, ALL = 10, 2, 42
+ALONG, ACROSS, ALL = 10, 2, 40
 
 
 def fetch(*copies):
@@ -52,8 +52,7 @@
     out_ref[...] = jnp.broadcast_to(ordered[None], out_ref.shape)
 
 
-def tokens_kernel(lat_hbm, rope_hbm, _, out_ref, lat_ref, rope_ref, sems):
-    fetch((lat_hbm, lat_ref, sems.at[0]), (rope_hbm, rope_ref, sems.at[1]))
+def put_tokens(lat_ref, rope_ref, out_ref):
     steps, requests, lat = lat_ref.shape
     rope = rope_ref.shape[2]
     rows = steps * requests
@@ -85,20 +84,23 @@
 
 
 def prepare_kernel(
-    scale, place_ref, length_ref, qr_hbm, rope_hbm, keys_hbm, uv_hbm, _,
-    bias_ref, own_ref, keys_ref, uv_own_ref, qr_ref, rope_ref, sems,
+    scale, place_ref, length_hbm, qr_hbm, rope_hbm, keys_hbm, uv_hbm, lat_new_hbm, rope_new_hbm, _,
+    bias_ref, own_ref, keys_ref, uv_own_ref, token_ref,
+    length_ref, qr_ref, rope_ref, lat_new_ref, rope_new_ref, sems,
 ):
     steps, requests, heads, ropes = qr_ref.shape
     shard = place_ref[0]
     owner = shard // (requests // (4 // steps))
     pairs = [
-        (rope_hbm, rope_ref), (qr_hbm, qr_ref), (keys_hbm, keys_ref), (uv_hbm.at[owner], uv_own_ref),
+        (lat_new_hbm, lat_new_ref), (rope_new_hbm, rope_new_ref), (length_hbm, length_ref),
+        (qr_hbm, qr_ref), (rope_hbm, rope_ref), (keys_hbm, keys_ref), (uv_hbm.at[owner], uv_own_ref),
     ]
     copies = [pltpu.make_async_copy(p, q, sems.at[i]) for i, (p, q) in enumerate(pairs)]
     for copy in copies:
         copy.start()
-    copies[0].wait()
-    copies[1].wait()
+    for copy in copies[:5]:
+        copy.wait()
+    put_tokens(lat_new_ref, rope_new_ref, token_ref)
     positions = rope_ref.shape[2]
     width = steps * heads
     lane = lax.broadcasted_iota(jnp.int32, (width, positions), 1) + shard * positions
@@ -120,7 +122,7 @@
     for g in range(groups):
         spread = (at == to - 8 + each * g) & (to >= 8) & (to < 8 + each)
         own_ref[g] = jnp.dot(mine, spread.astype(bf16), preferred_element_type=f32)
-    for copy in copies[2:]:
+    for copy in copies[5:]:
         copy.wait()
 
 
@@ -194,12 +196,15 @@
     steps, owned, _ = out_ref.shape
     groups = rope_ref.shape[0]
     parts = parts_ref[...].astype(f32)
+    shards = parts.shape[0]
     lanes = lax.broadcasted_iota(jnp.int32, parts.shape, 2)
     levels = jnp.sum(jnp.where(lanes < 3, parts, 0.0), axis=2, keepdims=True)
     lane = lanes[0]
     row = lax.broadcasted_iota(jnp.int32, (8, 1), 0)
     blocks = [
-        parts_ref[(g + groups - place_ref[1]) % groups + parts.shape[0] - shift].astype(f32)
+        parts_ref[
+            (holder((g + groups - place_ref[1]) % groups, shards // RINGS) + shards - shift) % shards
+        ].astype(f32)
         for g in range(groups)
     ]
     raw = jnp.concatenate(
@@ -245,10 +250,16 @@
     )
 
 
-def spread_tokens(block):
-    shards, groups = lax.axis_size("kv"), lax.axis_size("head")
+def holder(offset, size):
+    return offset % RINGS * size + ALONG - 1 + offset // RINGS
+
+
+def spread_tokens(block, size):
+    groups = lax.axis_size("head")
     pairs = [
-        (k * groups + (g + k) % groups, k * groups + g) for k in range(shards) for g in range(groups)
+        (holder(o, size) * groups + (g + o) % groups, holder(o, size) * groups + g)
+        for o in range(groups)
+        for g in range(groups)
     ]
     return lax.ppermute(block, ("kv", "head"), pairs)
 
@@ -297,24 +308,7 @@
     )(columns, *after)
 
 
-def tokens(new_latent, new_rope, after):
-    rows = new_latent.shape[0] * new_latent.shape[1]
-    return pl.pallas_call(
-        tokens_kernel,
-        out_shape=jax.ShapeDtypeStruct((rows, 128), bf16),
-        in_specs=[HBM, HBM, pl.BlockSpec(memory_space=pl.ANY)],
-        out_specs=VM,
-        scratch_shapes=[
-            pltpu.VMEM(new_latent.shape, bf16),
-            pltpu.VMEM(new_rope.shape, bf16),
-            pltpu.SemaphoreType.DMA((2,)),
-        ],
-        compiler_params=limit(4),
-        cost_estimate=cost(1 << 20, 1 << 16),
-    )(*pinned(pltpu.HBM, new_latent, new_rope), after)
-
-
-def prepare(scale, place, lengths, query_rope, cache_rope, cache_latent, uv_weight, after, groups):
+def prepare(scale, place, lengths, query_rope, cache_rope, cache_latent, uv_weight, lat_new, rope_new, after, groups):
     steps, requests, heads, _ = query_rope.shape
     positions = cache_rope.shape[2]
     return pl.pallas_call(
@@ -324,20 +318,25 @@
             near((groups, 8, 128), f32),
             near(cache_latent.shape, bf16),
             near(uv_weight.shape[1:], bf16),
+            jax.ShapeDtypeStruct((steps * requests, 128), bf16),
         ),
-        in_specs=[SM, SM] + [HBM] * 4 + [pl.BlockSpec(memory_space=pl.ANY)],
-        out_specs=(VM,) * 4,
+        in_specs=[SM] + [HBM] * 7 + [pl.BlockSpec(memory_space=pl.ANY)],
+        out_specs=(VM,) * 5,
         scratch_shapes=[
+            pltpu.SMEM(lengths.shape, jnp.int32),
             pltpu.VMEM(query_rope.shape, bf16),
             pltpu.VMEM(cache_rope.shape, bf16),
-            pltpu.SemaphoreType.DMA((4,)),
+            pltpu.VMEM(lat_new.shape, bf16),
+            pltpu.VMEM(rope_new.shape, bf16),
+            pltpu.SemaphoreType.DMA((7,)),
         ],
         compiler_params=limit(16),
         cost_estimate=cost(1 << 28, 1 << 22),
     )(
         place,
-        lengths,
-        *pinned(pltpu.HBM, query_rope, cache_rope, cache_latent, uv_weight),
+        *pinned(
+            pltpu.HBM, lengths, query_rope, cache_rope, cache_latent, uv_weight, lat_new, rope_new
+        ),
         after,
     )
 
@@ -396,10 +395,11 @@
     everyone = [[(i + ALL) % shards for i in range(shards)]]
     block = absorbed(query_nope, uk_weight, size)
     ring = exchange(block, along)
-    token = spread_tokens(tokens(new_latent, new_rope, block))
-    bias, ropes, keys, uv_own = prepare(
-        scale, place, lengths, query_rope, cache_rope, cache_latent, uv_weight, block, groups
-    )
+    bias, ropes, keys, uv_own, mine = prepare(
+        scale, place, lengths, query_rope, cache_rope, cache_latent, uv_weight,
+        new_latent, new_rope, block, groups,
+    )
+    token = spread_tokens(mine, size)
     queries = exchange(repeated(ring, ALONG, rings, ropes, token), across)
     parts, own = attend(scale, ACROSS, ALL, place, queries, keys, bias, uv_weight, token, shards)
     parts = exchange(parts, everyone)

time: 65 us -> 58 us (0.89)
  blocking collectives: 35.6 us -> 28.9 us
  waiting for transfers between devices: 0.77 us -> 2.36 us
  Pallas kernels: 9.08 us -> 8.19 us
  local copies, waits for them, and re-layouts: 0.66 us -> 0 us
    all_to_all x2, blocking collectives: 35.6 us -> 28.9 us  [exchange(): lax.all_to_all(array, 'kv', split_axis=0, concat_axis=0, tiled=True, axis...]
    all_to_all x1, waiting for transfers between devices: 0.77 us -> 2.36 us  [exchange(): lax.all_to_all(array, 'kv', split_axis=0, concat_axis=0, tiled=True, axis...]
    pallas_call x1 -> x0, Pallas kernels: 0.96 us -> none  [tokens(): pl.pallas_call(tokens_kernel, out_shape=jax.ShapeDtypeStruct((rows, 128),...]
    unnamed x2 -> x0, local copies, waits for them, and re-layouts: 0.66 us -> none
  transfers between devices with their start and end apart: 2 -> 2, of which waited for: 1 -> 1; matrix products, arithmetic and copies ran while one was open for 0% -> 0% of each run, Pallas kernels for 5% -> 4%
where the time goes in v3:
time: 58 us; the launch traced here: 57.3 us
  blocking collectives  28.9 us (50%)
  starting transfers between devices  17.7 us (31%)
  Pallas kernels  8.19 us (14%)
  waiting for transfers between devices  2.36 us (4%)
    all_to_all x2, blocking collectives, exchange(): lax.all_to_all(array, 'kv', split_axis=0, concat_axis=0, tiled=True, axis...  28.9 us
    all_to_all x1, starting transfers between devices, exchange(): lax.all_to_all(array, 'kv', split_axis=0, concat_axis=0, tiled=True, axis...  17.1 us
    pallas_call x1, Pallas kernels, attend(): pl.pallas_call(lambda *refs: attend_kernel(scale, turn, shift, *refs), ou...  2.66 us
    all_to_all x1, waiting for transfers between devices, exchange(): lax.all_to_all(array, 'kv', split_axis=0, concat_axis=0, tiled=True, axis...  2.36 us
    pallas_call x1, Pallas kernels, prepare(): pl.pallas_call(lambda *refs: prepare_kernel(scale, *refs), out_shape=(nea...  2.35 us
    pallas_call x1, Pallas kernels, absorbed(): pl.pallas_call(queries_kernel, out_shape=jax.ShapeDtypeStruct((copies, uk...  1.66 us
    pallas_call x1, Pallas kernels, merge(): pl.pallas_call(lambda *refs: merge_kernel(scale, shift, *refs), out_shape...  1.51 us
  transfers between devices with their start and end apart: 2, of which 1 were waited for; matrix products, arithmetic and copies ran while one was open for 0% of the time, Pallas kernels for 4%

profile of v3, /device:TPU:6, one launch (start us, length us, event | category | flops | bytes accessed | tf_op | source)
XLA Modules:
  0.0 57.3 jit_solution(8904860032197445077)
XLA Ops:
  0.0 1.7 %shard_map.91.refs_8_ = bf16[16,8,256]{2,1,0:T(8,128)(2,1)} custom-call(bf16[2,8,16,128]{3,2,1,0:T(8,128)(2,1)} %q_hbm.1, bf16[16,8,128]{2,1,0:T(8,128)(2,1)} %bitcast.3), custom_call_target="tpu_custom_call" | custom-call | tf_op jit(solution)/shard_map/pallas_call | solution.py:286
  1.7 17.1 %all-to-all-start = ((bf16[16,8,256]{2,1,0:T(8,128)(2,1)}), bf16[16,8,256]{2,1,0:T(8,128)(2,1)S(1)}, u32[]{:S(2)}, u32[]{:S(2)}) async-start(bf16[16,8,256]{2,1,0:T(8,128)(2,1)} %shard_map.91.refs_8_), calls=%async_computation | async-start | bytes 131072 | tf_op jit(solution)/shard_map/all_to_all | solution.py:248
  18.7 0.1 pad_add_fusion.refs_0_
  18.8 2.3 %shard_map.92 = (f32[256,256]{1,0:T(8,128)S(1)}, f32[8,8,128]{2,1,0:T(8,128)S(1)}, bf16[8,256,512]{2,1,0:T(8,128)(2,1)S(1)}, bf16[512,128]{1,0:T(8,128)(2,1)S(1)}, bf16[16,128]{1,0:T(8,128)(2,1)S(1)}) custom-call(s32[2]{0:T(128)S(1)} %pad_add_fusion.refs_0_, s32[8]{0:T(128)} %refs_1_.1, bf16[2,8,16,64]{3,2,1,0:T(8,128)(2,1)} %refs_2_.1, ...), custom_call_target="tpu_custom_call" | custom-call | flops 268435456 | bytes 4194304 | tf_op jit(solution)/shard_map/pallas_call | solution.py:314
  21.2 0.7 %collective-permute-start = (bf16[16,128]{1,0:T(8,128)(2,1)S(1)}, bf16[16,128]{1,0:T(8,128)(2,1)S(1)}, u32[]{:S(2)}, u32[]{:S(2)}) collective-permute-start(bf16[16,128]{1,0:T(8,128)(2,1)S(1)} %get-tuple-element.13), channel_id=1, source_target_pairs={{72,72},{73,73},{74,74},{75,75},{76,76},{77,77},{78,78},{79,79},{2... | collective-permute-start | bytes 12296 | tf_op jit(solution)/shard_map/ppermute | solution.py:264
  21.8 0.0 collective-permute-done.refs_2_.refs_5_
  21.9 2.4 %all-to-all-done.refs_0_ = bf16[16,8,256]{2,1,0:T(8,128)(2,1)S(1)} async-done(((bf16[16,8,256]{2,1,0:T(8,128)(2,1)}), bf16[16,8,256]{2,1,0:T(8,128)(2,1)S(1)}, u32[]{:S(2)}, u32[]{:S(2)}) %all-to-all-start) | async-done | bytes 65568 | tf_op jit(solution)/shard_map/all_to_all | solution.py:248
  24.2 8.8 %all_to_all.15.refs_1_ = bf16[4,128,256]{2,1,0:T(8,128)(2,1)S(1)} all-to-all(bf16[4,128,256]{2,1,0:T(8,128)(2,1)S(1)} %shard_map.93), channel_id=1, replica_groups={{256,384,0,128},{264,392,8,136},{272,400,16,144},{280,408,24,152},{288,..., dimensions={0} | all-to-all | bytes 524288 | tf_op jit(solution)/shard_map/all_to_all | solution.py:248
  33.0 2.7 %shard_map.94 = (bf16[64,8,128]{2,1,0:T(8,128)(2,1)S(1)}, f32[8,512]{1,0:T(8,128)S(1)}) custom-call(s32[2]{0:T(128)S(1)} %pad_add_fusion.refs_0_, bf16[4,128,256]{2,1,0:T(8,128)(2,1)S(1)} %all_to_all.15.refs_1_, bf16[8,256,512]{2,1,0:T(8,128)(2,1)S(1)} %get-tuple-element.14.refs_2_, f32[256,256]{1,0:T(8,128)S(1)} %get-tuple-element.15.refs_3_, ...), custom_call_target="tpu_custom_call" | custom-call | tf_op jit(solution)/shard_map/pallas_call | solution.py:347
  35.7 20.1 %all_to_all.16.refs_1_ = bf16[64,8,128]{2,1,0:T(8,128)(2,1)S(1)} all-to-all(bf16[64,8,128]{2,1,0:T(8,128)(2,1)S(1)} %get-tuple-element.16), channel_id=1, replica_groups={{320,328,336,344,352,360,368,376,384,392,400,408,416,424,432,440,448,45..., dimensions={0} | all-to-all | bytes 262144 | tf_op jit(solution)/shard_map/all_to_all | solution.py:248
  55.8 1.5 %shard_map.95 = bf16[2,2,128]{2,1,0:T(2,128)(2,1)} custom-call(s32[2]{0:T(128)S(1)} %pad_add_fusion.refs_0_, bf16[64,8,128]{2,1,0:T(8,128)(2,1)S(1)} %all_to_all.16.refs_1_, f32[8,512]{1,0:T(8,128)S(1)} %get-tuple-element.17.refs_2_, f32[8,8,128]{2,1,0:T(8,128)S(1)} %get-tuple-element.12.refs_1_.refs_3_, bf16[512,128]{1,0:T(8,128)(2,1)S(1)} %get-tuple-element.18.refs_4_), custom_call_target="tpu_custom_call" | custom-call | tf_op jit(solution)/shard_map/pallas_call | solution.py:366
  (1 shorter events, 0.0 us)
Async XLA Ops:
  1.7 22.5 %all-to-all-start = ((bf16[16,8,256]{2,1,0:T(8,128)(2,1)}), bf16[16,8,256]{2,1,0:T(8,128)(2,1)S(1)}, u32[]{:S(2)}, u32[]{:S(2)}) async-start(bf16[16,8,256]{2,1,0:T(8,128)(2,1)} %shard_map.91.refs_8_), calls=%async_computation | async-start | bytes 131072 | tf_op jit(solution)/shard_map/all_to_all | solution.py:248
  21.2 0.7 %collective-permute-start = (bf16[16,128]{1,0:T(8,128)(2,1)S(1)}, bf16[16,128]{1,0:T(8,128)(2,1)S(1)}, u32[]{:S(2)}, u32[]{:S(2)}) collective-permute-start(bf16[16,128]{1,0:T(8,128)(2,1)S(1)} %get-tuple-element.13), channel_id=1, source_target_pairs={{72,72},{73,73},{74,74},{75,75},{76,76},{77,77},{78,78},{79,79},{2... | collective-permute-start | bytes 12296 | tf_op jit(solution)/shard_map/ppermute | solution.py:264

commit v4 on v3

--- a/solution.py
+++ b/solution.py
@@ -177,19 +177,28 @@
     token = token_ref[...].astype(f32)
     copy.wait()
     upper = lax.broadcasted_iota(jnp.int32, (8, tile), 0) < 4
-    for h in range(heads):
+    shards = out_ref.shape[0]
+    for h in range(0, heads, 2):
         mixed = jnp.concatenate(
-            [mix_ref[c, pl.ds(h, each, stride=heads), :] for c in range(mix_ref.shape[0])], axis=1
+            [
+                jnp.concatenate(
+                    [mix_ref[c, pl.ds(i, each, stride=heads), :] for c in range(mix_ref.shape[0])], axis=1
+                )
+                for i in (h, h + 1)
+            ],
+            axis=0,
         ).astype(bf16)
-        stats = stat_ref[pl.ds(h, each, stride=heads), :] + token
-        projected = jnp.dot(mixed, uv_ref[h], preferred_element_type=f32)
-        for v in range(each // 8):
-            p = projected[v * 8 : (v + 1) * 8]
-            st = stats[v * 8 : (v + 1) * 8]
-            first = h * (each // 4) + 2 * v
-            shards = out_ref.shape[0]
-            out_ref[(first - shift) % shards] = jnp.where(upper, p, pltpu.roll(st, 4, 0)).astype(bf16)
-            out_ref[(first + 1 - shift) % shards] = jnp.where(upper, pltpu.roll(p, 4, 0), st).astype(bf16)
+        both = jnp.concatenate([uv_ref[h], uv_ref[h + 1]], axis=1)
+        result = jnp.dot(mixed, both, preferred_element_type=f32)
+        for i in range(2):
+            projected = result[i * each : (i + 1) * each, i * tile : (i + 1) * tile]
+            stats = stat_ref[pl.ds(h + i, each, stride=heads), :] + token
+            for v in range(each // 8):
+                p = projected[v * 8 : (v + 1) * 8]
+                st = stats[v * 8 : (v + 1) * 8]
+                first = (h + i) * (each // 4) + 2 * v
+                out_ref[(first - shift) % shards] = jnp.where(upper, p, pltpu.roll(st, 4, 0)).astype(bf16)
+                out_ref[(first + 1 - shift) % shards] = jnp.where(upper, pltpu.roll(p, 4, 0), st).astype(bf16)
 
 
 def merge_kernel(scale, shift, place_ref, parts_ref, q_ref, rope_ref, uv_ref, out_ref):

time: 58 us -> 57.9 us (level)
  no operation moved by 1% of the time
where the time goes in v4:
time: 57.9 us; the launch traced here: 57.2 us
  blocking collectives  28.9 us (50%)
  starting transfers between devices  17.7 us (31%)
  Pallas kernels  8.14 us (14%)
  waiting for transfers between devices  2.36 us (4%)
    all_to_all x2, blocking collectives, exchange(): lax.all_to_all(array, 'kv', split_axis=0, concat_axis=0, tiled=True, axis...  28.9 us
    all_to_all x1, starting transfers between devices, exchange(): lax.all_to_all(array, 'kv', split_axis=0, concat_axis=0, tiled=True, axis...  17.1 us
    pallas_call x1, Pallas kernels, attend(): pl.pallas_call(lambda *refs: attend_kernel(scale, turn, shift, *refs), ou...  2.6 us
    all_to_all x1, waiting for transfers between devices, exchange(): lax.all_to_all(array, 'kv', split_axis=0, concat_axis=0, tiled=True, axis...  2.36 us
    pallas_call x1, Pallas kernels, prepare(): pl.pallas_call(lambda *refs: prepare_kernel(scale, *refs), out_shape=(nea...  2.35 us
    pallas_call x1, Pallas kernels, absorbed(): pl.pallas_call(queries_kernel, out_shape=jax.ShapeDtypeStruct((copies, uk...  1.66 us
    pallas_call x1, Pallas kernels, merge(): pl.pallas_call(lambda *refs: merge_kernel(scale, shift, *refs), out_shape...  1.51 us
  transfers between devices with their start and end apart: 2, of which 1 were waited for; matrix products, arithmetic and copies ran while one was open for 0% of the time, Pallas kernels for 4%

profile of v4, /device:TPU:6, one launch (start us, length us, event | category | flops | bytes accessed | tf_op | source)
XLA Modules:
  0.0 57.2 jit_solution(6142591578370377452)
XLA Ops:
  0.0 1.7 %shard_map.91.refs_8_ = bf16[16,8,256]{2,1,0:T(8,128)(2,1)} custom-call(bf16[2,8,16,128]{3,2,1,0:T(8,128)(2,1)} %q_hbm.1, bf16[16,8,128]{2,1,0:T(8,128)(2,1)} %bitcast.3), custom_call_target="tpu_custom_call" | custom-call | tf_op jit(solution)/shard_map/pallas_call | solution.py:295
  1.7 17.1 %all-to-all-start = ((bf16[16,8,256]{2,1,0:T(8,128)(2,1)}), bf16[16,8,256]{2,1,0:T(8,128)(2,1)S(1)}, u32[]{:S(2)}, u32[]{:S(2)}) async-start(bf16[16,8,256]{2,1,0:T(8,128)(2,1)} %shard_map.91.refs_8_), calls=%async_computation | async-start | bytes 131072 | tf_op jit(solution)/shard_map/all_to_all | solution.py:257
  18.7 0.1 pad_add_fusion.refs_0_
  18.8 2.3 %shard_map.92 = (f32[256,256]{1,0:T(8,128)S(1)}, f32[8,8,128]{2,1,0:T(8,128)S(1)}, bf16[8,256,512]{2,1,0:T(8,128)(2,1)S(1)}, bf16[512,128]{1,0:T(8,128)(2,1)S(1)}, bf16[16,128]{1,0:T(8,128)(2,1)S(1)}) custom-call(s32[2]{0:T(128)S(1)} %pad_add_fusion.refs_0_, s32[8]{0:T(128)} %refs_1_.1, bf16[2,8,16,64]{3,2,1,0:T(8,128)(2,1)} %refs_2_.1, ...), custom_call_target="tpu_custom_call" | custom-call | flops 268435456 | bytes 4194304 | tf_op jit(solution)/shard_map/pallas_call | solution.py:323
  21.2 0.7 %collective-permute-start = (bf16[16,128]{1,0:T(8,128)(2,1)S(1)}, bf16[16,128]{1,0:T(8,128)(2,1)S(1)}, u32[]{:S(2)}, u32[]{:S(2)}) collective-permute-start(bf16[16,128]{1,0:T(8,128)(2,1)S(1)} %get-tuple-element.13), channel_id=1, source_target_pairs={{72,72},{73,73},{74,74},{75,75},{76,76},{77,77},{78,78},{79,79},{2... | collective-permute-start | bytes 12296 | tf_op jit(solution)/shard_map/ppermute | solution.py:273
  21.8 0.0 collective-permute-done.refs_2_.refs_5_
  21.9 2.4 %all-to-all-done.refs_0_ = bf16[16,8,256]{2,1,0:T(8,128)(2,1)S(1)} async-done(((bf16[16,8,256]{2,1,0:T(8,128)(2,1)}), bf16[16,8,256]{2,1,0:T(8,128)(2,1)S(1)}, u32[]{:S(2)}, u32[]{:S(2)}) %all-to-all-start) | async-done | bytes 65568 | tf_op jit(solution)/shard_map/all_to_all | solution.py:257
  24.2 8.8 %all_to_all.15.refs_1_ = bf16[4,128,256]{2,1,0:T(8,128)(2,1)S(1)} all-to-all(bf16[4,128,256]{2,1,0:T(8,128)(2,1)S(1)} %shard_map.93), channel_id=1, replica_groups={{256,384,0,128},{264,392,8,136},{272,400,16,144},{280,408,24,152},{288,..., dimensions={0} | all-to-all | bytes 524288 | tf_op jit(solution)/shard_map/all_to_all | solution.py:257
  33.0 2.6 %shard_map.94 = (bf16[64,8,128]{2,1,0:T(8,128)(2,1)S(1)}, f32[8,512]{1,0:T(8,128)S(1)}) custom-call(s32[2]{0:T(128)S(1)} %pad_add_fusion.refs_0_, bf16[4,128,256]{2,1,0:T(8,128)(2,1)S(1)} %all_to_all.15.refs_1_, bf16[8,256,512]{2,1,0:T(8,128)(2,1)S(1)} %get-tuple-element.14.refs_2_, f32[256,256]{1,0:T(8,128)S(1)} %get-tuple-element.15.refs_3_, ...), custom_call_target="tpu_custom_call" | custom-call | tf_op jit(solution)/shard_map/pallas_call | solution.py:356
  35.6 20.1 %all_to_all.16.refs_1_ = bf16[64,8,128]{2,1,0:T(8,128)(2,1)S(1)} all-to-all(bf16[64,8,128]{2,1,0:T(8,128)(2,1)S(1)} %get-tuple-element.16), channel_id=1, replica_groups={{320,328,336,344,352,360,368,376,384,392,400,408,416,424,432,440,448,45..., dimensions={0} | all-to-all | bytes 262144 | tf_op jit(solution)/shard_map/all_to_all | solution.py:257
  55.7 1.5 %shard_map.95 = bf16[2,2,128]{2,1,0:T(2,128)(2,1)} custom-call(s32[2]{0:T(128)S(1)} %pad_add_fusion.refs_0_, bf16[64,8,128]{2,1,0:T(8,128)(2,1)S(1)} %all_to_all.16.refs_1_, f32[8,512]{1,0:T(8,128)S(1)} %get-tuple-element.17.refs_2_, f32[8,8,128]{2,1,0:T(8,128)S(1)} %get-tuple-element.12.refs_1_.refs_3_, bf16[512,128]{1,0:T(8,128)(2,1)S(1)} %get-tuple-element.18.refs_4_), custom_call_target="tpu_custom_call" | custom-call | tf_op jit(solution)/shard_map/pallas_call | solution.py:375
  (1 shorter events, 0.0 us)
Async XLA Ops:
  1.7 22.5 %all-to-all-start = ((bf16[16,8,256]{2,1,0:T(8,128)(2,1)}), bf16[16,8,256]{2,1,0:T(8,128)(2,1)S(1)}, u32[]{:S(2)}, u32[]{:S(2)}) async-start(bf16[16,8,256]{2,1,0:T(8,128)(2,1)} %shard_map.91.refs_8_), calls=%async_computation | async-start | bytes 131072 | tf_op jit(solution)/shard_map/all_to_all | solution.py:257
  21.2 0.7 %collective-permute-start = (bf16[16,128]{1,0:T(8,128)(2,1)S(1)}, bf16[16,128]{1,0:T(8,128)(2,1)S(1)}, u32[]{:S(2)}, u32[]{:S(2)}) collective-permute-start(bf16[16,128]{1,0:T(8,128)(2,1)S(1)} %get-tuple-element.13), channel_id=1, source_target_pairs={{72,72},{73,73},{74,74},{75,75},{76,76},{77,77},{78,78},{79,79},{2... | collective-permute-start | bytes 12296 | tf_op jit(solution)/shard_map/ppermute | solution.py:273

commit v5 on v4

--- a/solution.py
+++ b/solution.py
@@ -16,7 +16,7 @@
 SM = pl.BlockSpec(memory_space=pltpu.SMEM)
 HBM = pl.BlockSpec(memory_space=pltpu.HBM)
 RINGS = 4
-ALONG, ACROSS, ALL = 10, 2, 40
+ALONG, ACROSS, ALL = 10, 2, 41
 
 
 def fetch(*copies):

time: 57.9 us -> 58 us (level)
  no operation moved by 1% of the time
where the time goes in v5:
time: 58 us; the launch traced here: 57.3 us
  blocking collectives  29 us (50%)
  starting transfers between devices  17.7 us (31%)
  Pallas kernels  8.14 us (14%)
  waiting for transfers between devices  2.36 us (4%)
    all_to_all x2, blocking collectives, exchange(): lax.all_to_all(array, 'kv', split_axis=0, concat_axis=0, tiled=True, axis...  29 us
    all_to_all x1, starting transfers between devices, exchange(): lax.all_to_all(array, 'kv', split_axis=0, concat_axis=0, tiled=True, axis...  17.1 us
    pallas_call x1, Pallas kernels, attend(): pl.pallas_call(lambda *refs: attend_kernel(scale, turn, shift, *refs), ou...  2.61 us
    all_to_all x1, waiting for transfers between devices, exchange(): lax.all_to_all(array, 'kv', split_axis=0, concat_axis=0, tiled=True, axis...  2.36 us
    pallas_call x1, Pallas kernels, prepare(): pl.pallas_call(lambda *refs: prepare_kernel(scale, *refs), out_shape=(nea...  2.35 us
    pallas_call x1, Pallas kernels, absorbed(): pl.pallas_call(queries_kernel, out_shape=jax.ShapeDtypeStruct((copies, uk...  1.66 us
    pallas_call x1, Pallas kernels, merge(): pl.pallas_call(lambda *refs: merge_kernel(scale, shift, *refs), out_shape...  1.51 us
  transfers between devices with their start and end apart: 2, of which 1 were waited for; matrix products, arithmetic and copies ran while one was open for 0% of the time, Pallas kernels for 4%

profile of v5, /device:TPU:6, one launch (start us, length us, event | category | flops | bytes accessed | tf_op | source)
XLA Modules:
  0.0 57.3 jit_solution(2870192244203629114)
XLA Ops:
  0.0 1.7 %shard_map.91.refs_8_ = bf16[16,8,256]{2,1,0:T(8,128)(2,1)} custom-call(bf16[2,8,16,128]{3,2,1,0:T(8,128)(2,1)} %q_hbm.1, bf16[16,8,128]{2,1,0:T(8,128)(2,1)} %bitcast.3), custom_call_target="tpu_custom_call" | custom-call | tf_op jit(solution)/shard_map/pallas_call | solution.py:295
  1.7 17.1 %all-to-all-start = ((bf16[16,8,256]{2,1,0:T(8,128)(2,1)}), bf16[16,8,256]{2,1,0:T(8,128)(2,1)S(1)}, u32[]{:S(2)}, u32[]{:S(2)}) async-start(bf16[16,8,256]{2,1,0:T(8,128)(2,1)} %shard_map.91.refs_8_), calls=%async_computation | async-start | bytes 131072 | tf_op jit(solution)/shard_map/all_to_all | solution.py:257
  18.7 0.1 pad_add_fusion.refs_0_
  18.8 2.3 %shard_map.92 = (f32[256,256]{1,0:T(8,128)S(1)}, f32[8,8,128]{2,1,0:T(8,128)S(1)}, bf16[8,256,512]{2,1,0:T(8,128)(2,1)S(1)}, bf16[512,128]{1,0:T(8,128)(2,1)S(1)}, bf16[16,128]{1,0:T(8,128)(2,1)S(1)}) custom-call(s32[2]{0:T(128)S(1)} %pad_add_fusion.refs_0_, s32[8]{0:T(128)} %refs_1_.1, bf16[2,8,16,64]{3,2,1,0:T(8,128)(2,1)} %refs_2_.1, ...), custom_call_target="tpu_custom_call" | custom-call | flops 268435456 | bytes 4194304 | tf_op jit(solution)/shard_map/pallas_call | solution.py:323
  21.2 0.7 %collective-permute-start = (bf16[16,128]{1,0:T(8,128)(2,1)S(1)}, bf16[16,128]{1,0:T(8,128)(2,1)S(1)}, u32[]{:S(2)}, u32[]{:S(2)}) collective-permute-start(bf16[16,128]{1,0:T(8,128)(2,1)S(1)} %get-tuple-element.13), channel_id=1, source_target_pairs={{72,72},{73,73},{74,74},{75,75},{76,76},{77,77},{78,78},{79,79},{2... | collective-permute-start | bytes 12296 | tf_op jit(solution)/shard_map/ppermute | solution.py:273
  21.8 0.0 collective-permute-done.refs_2_.refs_5_
  21.9 2.4 %all-to-all-done.refs_0_ = bf16[16,8,256]{2,1,0:T(8,128)(2,1)S(1)} async-done(((bf16[16,8,256]{2,1,0:T(8,128)(2,1)}), bf16[16,8,256]{2,1,0:T(8,128)(2,1)S(1)}, u32[]{:S(2)}, u32[]{:S(2)}) %all-to-all-start) | async-done | bytes 65568 | tf_op jit(solution)/shard_map/all_to_all | solution.py:257
  24.2 8.8 %all_to_all.15.refs_1_ = bf16[4,128,256]{2,1,0:T(8,128)(2,1)S(1)} all-to-all(bf16[4,128,256]{2,1,0:T(8,128)(2,1)S(1)} %shard_map.93), channel_id=1, replica_groups={{256,384,0,128},{264,392,8,136},{272,400,16,144},{280,408,24,152},{288,..., dimensions={0} | all-to-all | bytes 524288 | tf_op jit(solution)/shard_map/all_to_all | solution.py:257
  33.0 2.6 %shard_map.94 = (bf16[64,8,128]{2,1,0:T(8,128)(2,1)S(1)}, f32[8,512]{1,0:T(8,128)S(1)}) custom-call(s32[2]{0:T(128)S(1)} %pad_add_fusion.refs_0_, bf16[4,128,256]{2,1,0:T(8,128)(2,1)S(1)} %all_to_all.15.refs_1_, bf16[8,256,512]{2,1,0:T(8,128)(2,1)S(1)} %get-tuple-element.14.refs_2_, f32[256,256]{1,0:T(8,128)S(1)} %get-tuple-element.15.refs_3_, ...), custom_call_target="tpu_custom_call" | custom-call | tf_op jit(solution)/shard_map/pallas_call | solution.py:356
  35.6 20.2 %all_to_all.16.refs_1_ = bf16[64,8,128]{2,1,0:T(8,128)(2,1)S(1)} all-to-all(bf16[64,8,128]{2,1,0:T(8,128)(2,1)S(1)} %get-tuple-element.16), channel_id=1, replica_groups={{328,336,344,352,360,368,376,384,392,400,408,416,424,432,440,448,456,46..., dimensions={0} | all-to-all | bytes 262144 | tf_op jit(solution)/shard_map/all_to_all | solution.py:257
  55.8 1.5 %shard_map.95 = bf16[2,2,128]{2,1,0:T(2,128)(2,1)} custom-call(s32[2]{0:T(128)S(1)} %pad_add_fusion.refs_0_, bf16[64,8,128]{2,1,0:T(8,128)(2,1)S(1)} %all_to_all.16.refs_1_, f32[8,512]{1,0:T(8,128)S(1)} %get-tuple-element.17.refs_2_, f32[8,8,128]{2,1,0:T(8,128)S(1)} %get-tuple-element.12.refs_1_.refs_3_, bf16[512,128]{1,0:T(8,128)(2,1)S(1)} %get-tuple-element.18.refs_4_), custom_call_target="tpu_custom_call" | custom-call | tf_op jit(solution)/shard_map/pallas_call | solution.py:375
  (1 shorter events, 0.0 us)
Async XLA Ops:
  1.7 22.5 %all-to-all-start = ((bf16[16,8,256]{2,1,0:T(8,128)(2,1)}), bf16[16,8,256]{2,1,0:T(8,128)(2,1)S(1)}, u32[]{:S(2)}, u32[]{:S(2)}) async-start(bf16[16,8,256]{2,1,0:T(8,128)(2,1)} %shard_map.91.refs_8_), calls=%async_computation | async-start | bytes 131072 | tf_op jit(solution)/shard_map/all_to_all | solution.py:257
  21.2 0.7 %collective-permute-start = (bf16[16,128]{1,0:T(8,128)(2,1)S(1)}, bf16[16,128]{1,0:T(8,128)(2,1)S(1)}, u32[]{:S(2)}, u32[]{:S(2)}) collective-permute-start(bf16[16,128]{1,0:T(8,128)(2,1)S(1)} %get-tuple-element.13), channel_id=1, source_target_pairs={{72,72},{73,73},{74,74},{75,75},{76,76},{77,77},{78,78},{79,79},{2... | collective-permute-start | bytes 12296 | tf_op jit(solution)/shard_map/ppermute | solution.py:273
